TPU v7x, 512 devices: a whole 4x4x16 slice. The times are simulated.
512 devices in a mesh: dp: 32 (over z, x_hi), tensor: 16 (over x_lo, y, core).
Axes of the slice: x: 4 (x_hi: 2, x_lo: 2; x = x_hi * 2 + x_lo), y: 4, z: 16, core: 2. Of those that a mesh axis runs over, the one named last changes fastest.
Arguments:
- tokens: bfloat16 [1024, 16384], P('dp', 'tensor'), may hold values from -6 to 6
- up_weight: bfloat16 [26624, 16384], P('dp', 'tensor'), may hold values from -0.046875 to 0.046875
- angles: float32 [4, 16384], P(None, 'tensor'), may hold values from -0.6 to 0.6
- pair_order: int32 [4, 1024], replicated, may hold values from 0 to 1023, each once within a row
- cotangent: bfloat16 [1024, 26624], P('tensor', 'dp'), may hold values from -0.14648438 to 0.14648438
Outputs:
- projected: bfloat16 [1024, 26624], P('tensor', 'dp')
- angle_grads: float32 [4, 16384], P(None, 'tensor')
Inputs may be any that keep to these rules, and one draw needn't show every extreme that they name: Each row of pair_order is a permutation of 0 .. 1023.
All inputs are finite; a program needn't handle non-finite values.
Results may differ from a plain program's by a relative error of at most 0.025.
Values may be sent and summed in bfloat16 or wider, within the bound.
No kernel may reach another device: no remote copies, remote signals or barrier semaphores. Data moves between devices by JAX's collectives and lax.ppermute only.
A program may use at most 128 MiB of HBM per device.

v0:
```python
import jax
import jax.numpy as jnp
from jax import lax
from jax.sharding import PartitionSpec as P


def partner_2(array, axis, stride):
    return lax.ppermute(array, axis, [(i, i ^ 1 << stride) for i in range(lax.axis_size(axis))])


def rotate_pair(lower_rows, upper_rows, pair_row, lower_angle, upper_angle):
    partner = jnp.take(upper_rows, pair_row, axis=-1)
    turned = lower_angle + jnp.take(upper_angle, pair_row, axis=-1)
    cosine = jnp.cos(turned)
    sine_part = jnp.sin(turned)
    new_lower = cosine * lower_rows - sine_part * partner
    new_partner = sine_part * lower_rows + cosine * partner
    return (new_lower, new_partner, turned)


def pair_gradient(new_lower, new_partner, grad_lower, grad_upper, pair_row, turned):
    cosine = jnp.cos(turned)
    sine_part = jnp.sin(turned)
    partner_grad = jnp.take(grad_upper, pair_row, axis=-1)
    angle_grad = jnp.sum(partner_grad * new_lower - grad_lower * new_partner, axis=0)
    before_lower = cosine * grad_lower + sine_part * partner_grad
    before_partner = cosine * partner_grad - sine_part * grad_lower
    return (angle_grad, before_lower, before_partner)


def per_device(tokens, up_weight, angles, pair_order, cotangent):
    groups = lax.axis_size("tensor")
    bit_count = groups.bit_length() - 1
    sections = pair_order.shape[0]
    section_bits = [(bit_count - 1 - factor) % bit_count for factor in range(sections)]
    inverses = [jnp.argsort(pair_order[factor]) for factor in range(sections)]
    position = lax.axis_index("tensor")
    stored = []
    current = tokens.astype(jnp.float32)
    for factor in range(sections):
        section_bit = section_bits[factor]
        stride = 2**section_bit
        is_lower = position // stride % 2 == 0
        own_angle = angles[factor]
        partner, partner_angle = (
            partner_2(current.astype(jnp.bfloat16), "tensor", section_bit).astype(current.dtype),
            partner_2(own_angle.astype(jnp.bfloat16), "tensor", section_bit).astype(
                own_angle.dtype
            ),
        )
        lower_rows = jnp.where(is_lower, current, partner)
        upper_rows = jnp.where(is_lower, partner, current)
        lower_angle = jnp.where(is_lower, own_angle, partner_angle)
        upper_angle = jnp.where(is_lower, partner_angle, own_angle)
        new_lower, new_partner, turned = rotate_pair(
            lower_rows, upper_rows, pair_order[factor], lower_angle, upper_angle
        )
        stored.append((is_lower, new_lower, new_partner, turned))
        current = jnp.where(is_lower, new_lower, jnp.take(new_partner, inverses[factor], axis=-1))
    rotated = current.astype(jnp.bfloat16)
    token_all = lax.all_gather(rotated, "dp", axis=0, tiled=True)
    row_block = token_all
    summed = lax.psum_scatter(
        lax.dot_general(
            row_block, up_weight, (((1,), (1,)), ((), ())), preferred_element_type=jnp.float32
        ).astype(jnp.bfloat16),
        "tensor",
        scatter_dimension=0,
        tiled=True,
    )
    cotangent_all = lax.all_gather(cotangent, "tensor", axis=0, tiled=True)
    row_block = cotangent_all
    gradient = lax.psum_scatter(
        jnp.dot(row_block, up_weight, preferred_element_type=jnp.float32).astype(jnp.bfloat16),
        "dp",
        scatter_dimension=0,
        tiled=True,
    ).astype(jnp.float32)
    factor_sums = [None] * sections
    current = gradient
    for factor in reversed(range(sections)):
        is_lower, new_lower, new_partner, turned = stored[factor]
        partner = partner_2(current.astype(jnp.bfloat16), "tensor", section_bits[factor]).astype(
            current.dtype
        )
        grad_lower = jnp.where(is_lower, current, partner)
        grad_upper = jnp.where(is_lower, partner, current)
        angle_grad, before_lower, before_partner = pair_gradient(
            new_lower, new_partner, grad_lower, grad_upper, pair_order[factor], turned
        )
        factor_sums[factor] = jnp.where(
            is_lower, angle_grad, jnp.take(angle_grad, inverses[factor], axis=-1)
        )
        current = jnp.where(
            is_lower, before_lower, jnp.take(before_partner, inverses[factor], axis=-1)
        )
    own_sums = jnp.stack(factor_sums)
    angle_grads = lax.psum(own_sums, "dp")
    return (summed, angle_grads)


def solution(mesh):
    placed = (P("dp", "tensor"), P("dp", "tensor"), P(None, "tensor"), P(), P("tensor", "dp"))
    return jax.shard_map(
        per_device,
        mesh=mesh,
        in_specs=placed,
        out_specs=(P("tensor", "dp"), P(None, "tensor")),
        check_vma=False,
    )
```

profile of v0, /device:TPU:24, one launch (start us, length us, event | category | flops | bytes accessed | tf_op | source)
XLA Modules:
  0.0 1170.0 jit_solution(973135956580557358)
XLA Ops:
  8.0 0.9 fusion.53
  8.9 1.9 collective-permute-start
  10.8 2.7 collective-permute-start.1
  13.5 8.2 collective-permute-start.2
  21.7 1.9 collective-permute-start.3
  23.6 3.9 collective-permute-start.4
  27.6 0.9 fusion.54
  28.5 4.4 sort.62
  32.9 4.4 sort.61
  37.3 4.4 sort.60
  41.6 4.4 sort.59
  46.0 9.9 all-gather.5.cloned.1.call-done
  55.9 5.2 convolution_convert_fusion
  63.1 4.5 gather_fusion
  67.7 4.5 gather_fusion.1
  72.2 4.5 gather_fusion.2
  76.8 4.5 gather_fusion.3
  82.2 650.7 %reduce-scatter.5.cloned.1.call-done = bf16[32,1024]{1,0:T(8,128)(2,1)} async-done(((bf16[1024,1024]{1,0:T(8,128)(2,1)}), bf16[32,1024]{1,0:T(8,128)(2,1)}) %reduce-scatter.5.cloned.1.call-update) | async-done | bytes 65552 | tf_op jit(solution)/shard_map/reduce_scatter | solution.py:73
  732.9 2.0 collective-permute-start.8
  735.0 1.4 collective-permute-done.8
  737.5 2.8 gather_fusion.12
  740.7 2.8 gather_fusion.13
  743.8 2.7 collective-permute-start.9
  747.1 2.8 collective-permute-done.9
  750.2 2.8 gather_fusion.14
  753.4 2.8 gather_fusion.15
  756.5 3.3 collective-permute-start.10
  760.5 3.7 collective-permute-done.10
  764.4 3.3 gather_fusion.16
  768.8 4.3 gather_fusion.17
  773.1 1.2 copy.64
  775.1 2.5 collective-permute-start.11
  778.7 4.3 gather_fusion.4
  783.0 1.2 copy.38
  784.9 1.1 copy.65
  786.0 4.0 gather_fusion.18
  790.0 1.2 copy.66
  791.3 1.0 fusion.2
  792.4 4.3 gather_fusion.5
  796.8 1.2 copy.40
  798.0 4.5 gather_fusion.19
  803.2 0.9 fusion.52
  804.1 3.3 collective-permute-start.5
  807.4 4.4 collective-permute-done.5
  812.0 4.0 gather_fusion.6
  816.0 1.2 copy.42
  818.0 1.1 copy.43
  819.1 4.0 gather_fusion.7
  823.1 1.2 copy.44
  824.4 2.7 collective-permute-start.6
  827.2 3.4 collective-permute-done.6
  830.8 2.8 gather_fusion.8
  834.9 4.3 gather_fusion.9
  839.2 1.2 copy.48
  840.5 2.1 collective-permute-start.7
  842.6 1.0 collective-permute-done.7
  843.9 2.8 gather_fusion.10
  847.2 3.2 gather_fusion.11
  851.3 148.2 %all-gather.3.cloned.1.call-done = bf16[1024,1024]{1,0:T(8,128)(2,1)} async-done(((bf16[32,1024]{1,0:T(8,128)(2,1)}), bf16[1024,1024]{1,0:T(8,128)(2,1)}) %all-gather.3.cloned.1.call-update) | async-done | bytes 2097168 | tf_op jit(solution)/shard_map/all_gather | solution.py:61
  999.5 5.2 convolution_convert_fusion.1
  1005.4 4.5 gather_fusion.20
  1010.0 4.5 gather_fusion.21
  1014.5 4.5 gather_fusion.22
  1019.1 144.3 %psum.7 = f32[4,1024]{1,0:T(4,128)} all-reduce(f32[4,1024]{1,0:T(4,128)S(1)} %pad_maximum_fusion), channel_id=1, replica_groups=mesh['dp'=32,'tensor'=16] {'dp'}, use_global_device_ids=true, to_apply=%region_10.13 | all-reduce | flops 4096 | bytes 32768 | tf_op jit(solution)/shard_map/psum | solution.py:98
  (192 shorter events, 16.7 us)
Async XLA Ops:
  7.2 48.7 %copy-start = (bf16[832,1024]{1,0:T(8,128)(2,1)S(1)}, bf16[832,1024]{1,0:T(8,128)(2,1)}, u32[]{:S(2)}) copy-start(bf16[832,1024]{1,0:T(8,128)(2,1)} %param.10) | copy-start | bytes 5111812
  7.2 48.7 %all-gather.5.cloned.1.call-start = ((), (), s32[]{:S(2)}) async-start(), calls=%async_computation.4 | async-start | bytes 1949696 | tf_op jit(solution)/shard_map/all_gather | solution.py:71
  7.9 725.0 %reduce-scatter.5.cloned.1.call-start = ((), (), s32[]{:S(2)}) async-start(), calls=%async_computation.5 | async-start | bytes 2162688 | tf_op jit(solution)/shard_map/reduce_scatter | solution.py:73
  8.9 54.2 %collective-permute-start = (bf16[1024]{0:T(1024)(128)(2,1)S(1)}, bf16[1024]{0:T(1024)(128)(2,1)S(1)}, u32[]{:S(2)}, u32[]{:S(2)}) collective-permute-start(bf16[1024]{0:T(1024)(128)(2,1)S(1)} %convert_element_type.83), channel_id=1, source_target_pairs={{0,1},{1,0},{2,3},{3,2},{4,5},{5,4},{6,7},{7,6},{8,9},{9,8},{10,11... | collective-permute-start | bytes 6152 | tf_op jit(solution)/shard_map/ppermute | solution.py:8
  10.8 52.3 %collective-permute-start.1 = (bf16[1024]{0:T(1024)(128)(2,1)S(1)}, bf16[1024]{0:T(1024)(128)(2,1)S(1)}, u32[]{:S(2)}, u32[]{:S(2)}) collective-permute-start(bf16[1024]{0:T(1024)(128)(2,1)S(1)} %convert_element_type.85), channel_id=1, source_target_pairs={{0,2},{1,3},{2,0},{3,1},{4,6},{5,7},{6,4},{7,5},{8,10},{9,11},{10,... | collective-permute-start | bytes 6152 | tf_op jit(solution)/shard_map/ppermute | solution.py:8
  13.5 49.6 %collective-permute-start.2 = (bf16[1024]{0:T(1024)(128)(2,1)S(1)}, bf16[1024]{0:T(1024)(128)(2,1)S(1)}, u32[]{:S(2)}, u32[]{:S(2)}) collective-permute-start(bf16[1024]{0:T(1024)(128)(2,1)S(1)} %convert_element_type.87), channel_id=1, source_target_pairs={{0,4},{1,5},{2,6},{3,7},{4,0},{5,1},{6,2},{7,3},{8,12},{9,13},{10,... | collective-permute-start | bytes 6152 | tf_op jit(solution)/shard_map/ppermute | solution.py:8
  21.7 55.0 %collective-permute-start.3 = (bf16[1024]{0:T(1024)(128)(2,1)S(1)}, bf16[1024]{0:T(1024)(128)(2,1)S(1)}, u32[]{:S(2)}, u32[]{:S(2)}) collective-permute-start(bf16[1024]{0:T(1024)(128)(2,1)S(1)} %convert_element_type.89), channel_id=1, source_target_pairs={{0,8},{1,9},{2,10},{3,11},{4,12},{5,13},{6,14},{7,15},{8,0},{9,1},... | collective-permute-start | bytes 6152 | tf_op jit(solution)/shard_map/ppermute | solution.py:8
  23.6 754.0 %collective-permute-start.4 = (bf16[32,1024]{1,0:T(8,128)(2,1)}, bf16[32,1024]{1,0:T(8,128)(2,1)}, u32[]{:S(2)}, u32[]{:S(2)}) collective-permute-start(bf16[32,1024]{1,0:T(8,128)(2,1)} %param.9), channel_id=1, source_target_pairs={{0,8},{1,9},{2,10},{3,11},{4,12},{5,13},{6,14},{7,15},{8,0},{9,1},... | collective-permute-start | bytes 196616 | tf_op jit(solution)/shard_map/ppermute | solution.py:8
  32.9 28.9 %copy-start.32 = (s32[1024]{0:T(1024)}, s32[1024]{0:T(1024)S(1)}, u32[]{:S(2)}) copy-start(s32[1024]{0:T(1024)S(1)} %get-tuple-element.11) | copy-start | bytes 12292
  37.2 24.5 %copy-start.34 = (s32[1024]{0:T(1024)}, s32[1024]{0:T(1024)S(1)}, u32[]{:S(2)}) copy-start(s32[1024]{0:T(1024)S(1)} %get-tuple-element.10) | copy-start | bytes 12292
  41.6 20.2 %copy-start.36 = (s32[1024]{0:T(1024)}, s32[1024]{0:T(1024)S(1)}, u32[]{:S(2)}) copy-start(s32[1024]{0:T(1024)S(1)} %get-tuple-element.9) | copy-start | bytes 12292
  46.0 16.5 %copy-start.41 = (s32[1024]{0:T(1024)}, s32[1024]{0:T(1024)S(1)}, u32[]{:S(2)}) copy-start(s32[1024]{0:T(1024)S(1)} %get-tuple-element.8) | copy-start | bytes 12292
  46.0 697.7 %copy-start.44 = (pred[1024]{0:T(1024)(128)(4,1)}, pred[1024]{0:T(1024)(128)(4,1)S(1)}, u32[]{:S(2)}) copy-start(pred[1024]{0:T(1024)(128)(4,1)S(1)} %compare_and_fusion) | copy-start | bytes 3076
  61.1 938.4 %all-gather.3.cloned.1.call-start = ((), (), s32[]{:S(2)}) async-start(), calls=%async_computation.2 | async-start | bytes 2162688 | tf_op jit(solution)/shard_map/all_gather | solution.py:61
  61.2 695.2 %copy-start.46 = (pred[1024]{0:T(1024)(128)(4,1)}, pred[1024]{0:T(1024)(128)(4,1)S(1)}, u32[]{:S(2)}) copy-start(pred[1024]{0:T(1024)(128)(4,1)S(1)} %compare_and_fusion.1) | copy-start | bytes 3076
  61.7 675.7 %copy-start.15 = (s32[1024]{0:T(1024)}, s32[1024]{0:T(1024)S(1)}, u32[]{:S(2)}) copy-start(s32[1024]{0:T(1024)S(1)} %fusion.28) | copy-start | bytes 12292
  61.8 678.9 %copy-start.9 = (s32[1024]{0:T(1024)}, s32[1024]{0:T(1024)S(1)}, u32[]{:S(2)}) copy-start(s32[1024]{0:T(1024)S(1)} %fusion.35) | copy-start | bytes 12292
  61.8 688.4 %copy-start.17 = (s32[1024]{0:T(1024)}, s32[1024]{0:T(1024)S(1)}, u32[]{:S(2)}) copy-start(s32[1024]{0:T(1024)S(1)} %fusion.29) | copy-start | bytes 12292
  61.8 691.6 %copy-start.11 = (s32[1024]{0:T(1024)}, s32[1024]{0:T(1024)S(1)}, u32[]{:S(2)}) copy-start(s32[1024]{0:T(1024)S(1)} %fusion.34) | copy-start | bytes 12292
  61.9 10.3 copy-start.19
  62.5 14.3 %copy-start.21 = (s32[1024]{0:T(1024)}, s32[1024]{0:T(1024)S(1)}, u32[]{:S(2)}) copy-start(s32[1024]{0:T(1024)S(1)} %fusion.31) | copy-start | bytes 12292
  81.4 662.4 %copy-start.24 = (pred[1024]{0:T(1024)(128)(4,1)}, pred[1024]{0:T(1024)(128)(4,1)S(1)}, u32[]{:S(2)}) copy-start(pred[1024]{0:T(1024)(128)(4,1)S(1)} %get-tuple-element.27) | copy-start | bytes 3076
  81.4 662.3 %copy-start.3 = (f32[1024]{0:T(1024)}, f32[1024]{0:T(1024)S(1)}, u32[]{:S(2)}) copy-start(f32[1024]{0:T(1024)S(1)} %fusion.42) | copy-start | bytes 12292
  81.5 675.0 %copy-start.26 = (pred[1024]{0:T(1024)(128)(4,1)}, pred[1024]{0:T(1024)(128)(4,1)S(1)}, u32[]{:S(2)}) copy-start(pred[1024]{0:T(1024)(128)(4,1)S(1)} %get-tuple-element.31) | copy-start | bytes 3076
  81.5 665.0 %copy-start.28 = (pred[1024]{0:T(1024)(128)(4,1)}, pred[1024]{0:T(1024)(128)(4,1)S(1)}, u32[]{:S(2)}) copy-start(pred[1024]{0:T(1024)(128)(4,1)S(1)} %get-tuple-element.35) | copy-start | bytes 3076
  82.2 677.7 %copy-start.39 = (pred[1024]{0:T(1024)(128)(4,1)}, pred[1024]{0:T(1024)(128)(4,1)S(1)}, u32[]{:S(2)}) copy-start(pred[1024]{0:T(1024)(128)(4,1)S(1)} %get-tuple-element.39) | copy-start | bytes 3076
  732.9 7.5 copy-start.1
  732.9 3.5 collective-permute-start.8
  735.0 21.4 %copy-start.5 = (f32[1024]{0:T(1024)}, f32[1024]{0:T(1024)S(1)}, u32[]{:S(2)}) copy-start(f32[1024]{0:T(1024)S(1)} %fusion.40) | copy-start | bytes 12292
  743.8 6.2 collective-permute-start.9
  756.4 11.5 copy-start.7
  756.5 7.7 collective-permute-start.10
  767.9 6.5 copy-start.29
  767.9 6.5 copy-start.48
  767.9 9.7 copy-start.2
  775.1 11.0 copy-start.22
  775.1 9.2 collective-permute-start.11
  792.2 5.8 copy-start.38
  798.0 4.6 copy-start.42
  798.0 5.2 copy-start.23
  798.0 5.2 copy-start.31
  798.0 5.2 copy-start.40
  798.0 14.0 %copy-start.20 = (s32[1024]{0:T(1024)S(1)}, s32[1024]{0:T(1024)}, u32[]{:S(2)}) copy-start(s32[1024]{0:T(1024)} %copy-done.19) | copy-start | bytes 12292
  802.6 14.7 %copy-start.8 = (f32[1024]{0:T(1024)S(1)}, f32[1024]{0:T(1024)}, u32[]{:S(2)}) copy-start(f32[1024]{0:T(1024)} %fusion.38) | copy-start | bytes 12292
  802.6 14.7 %copy-start.30 = (pred[1024]{0:T(1024)(128)(4,1)S(1)}, pred[1024]{0:T(1024)(128)(4,1)}, u32[]{:S(2)}) copy-start(pred[1024]{0:T(1024)(128)(4,1)} %copy-done.28) | copy-start | bytes 3076
  804.1 7.7 collective-permute-start.5
  811.8 7.3 copy-start.13
  816.0 8.3 copy-start.49
  819.1 11.7 copy-start.18
  824.4 6.2 collective-permute-start.6
  833.8 6.6 copy-start.6
  833.8 6.6 copy-start.27
  833.8 6.6 copy-start.47
  834.9 9.0 copy-start.16
  840.4 6.5 copy-start.4
  840.5 6.5 copy-start.25
  840.5 3.1 collective-permute-start.7
  843.9 6.6 copy-start.45
  851.3 312.2 %reduce-scatter.3.cloned.1.call-start = ((), (), s32[]{:S(2)}) async-start(), calls=%async_computation.3 | async-start | bytes 1949696 | tf_op jit(solution)/shard_map/reduce_scatter | solution.py:63
  1005.4 4.5 copy-start.37
  1005.4 4.6 copy-start.12
  1009.9 4.5 copy-start.35
  1014.5 4.6 copy-start.33
  1014.5 4.6 copy-start.43
  (2 other events, 4.2 us)
Sparse Core Ops, SparseCore 0:
  10.2 45.6 all-gather.4
  61.2 671.6 reduce-scatter.4
  851.4 148.0 all-gather.2
  1004.8 61.5 reduce-scatter.2
where the time goes:
time: 1170 us
  waiting for transfers between devices  826 us (71%)
  blocking collectives  144 us (12%)
  local copies, waits for them, and re-layouts  106 us (9%)
  starting transfers between devices  37.5 us (3%)
  other arithmetic  30.4 us (3%)
  between operations  15 us (1%)
    reduce_scatter x1, waiting for transfers between devices, per_device(): lax.psum_scatter(jnp.dot(row_block, up_weight, preferred_element_type=jnp...  651 us
    all_gather x1, waiting for transfers between devices, per_device(): token_all = lax.all_gather(rotated, 'dp', axis=0, tiled=True)  148 us
    psum x1, blocking collectives, per_device(): angle_grads = lax.psum(own_sums, 'dp')  144 us
    ppermute x12, starting transfers between devices, partner_2(): lax.ppermute(array, axis, [(i, i ^ 1 << stride) for i in range(lax.axis_s...  37.4 us
  transfers between devices with their start and end apart: 16, of which 9 were waited for; matrix products, arithmetic and copies ran while one was open for 8% of the time, Pallas kernels for 0%

commit v1 on v0

v1 whole, which is shorter than its diff:
```python
import functools

import jax
import jax.numpy as jnp
import numpy as np
from jax import lax
from jax.experimental import pallas as pl
from jax.experimental.pallas import tpu as pltpu
from jax.sharding import PartitionSpec as P

BF16 = jnp.bfloat16
F32 = jnp.float32
Z = "z"
TENSOR = ("xl", "y", "c")
NEAR = ("xl", "y")
PLANE = ("xh", "xl", "y", "c")
STEPS = (64, 32, 16, 8, 4, 2)


def all_to_all(array, axes):
    return lax.all_to_all(array, axes, 0, 0, tiled=True)


def split_two(value):
    high = value.astype(BF16)
    low = (value - high.astype(F32)).astype(BF16)
    return high, low


def permuted(value, matrix, transposed):
    rows = value.shape[0]
    both = jnp.concatenate(split_two(value), axis=0)
    dims = (((1,), (1 if transposed else 0,)), ((), ()))
    out = lax.dot_general(both, matrix, dims, preferred_element_type=F32)
    return out[:rows] + out[rows:]


def spread(matrix, value):
    high, low = split_two(value)
    dims = (((1,), (0,)), ((), ()))
    return lax.dot_general(matrix, high, dims, preferred_element_type=F32) + lax.dot_general(
        matrix, low, dims, preferred_element_type=F32
    )


def swap_groups(value, distance):
    rows = value.shape[0]
    if distance < 8:
        parts = [pltpu.roll(value[i : i + 8], 4, 0) for i in range(0, rows, 8)]
    else:
        parts = []
        for i in range(0, rows, 2 * distance):
            parts += [value[i + distance : i + 2 * distance], value[i : i + distance]]
    return jnp.concatenate(parts, axis=0)


def forward_kernel(bits, each, x_ref, low_ref, up_ref, order_ref, pick_ref, mask_ref,
                   z_ref, kept_ref, cos_ref, sin_ref, now):
    step = pl.program_id(0)

    @pl.when(step == 0)
    def _():
        now[...] = x_ref[...].astype(F32)

    order = order_ref[0]
    turned = low_ref[0] + permuted(up_ref[0], order, False)
    cosine = jnp.cos(turned)
    sine = jnp.sin(turned)
    cos_ref[0] = cosine
    sin_ref[0] = sine
    cos_rows = spread(pick_ref[0, 0], cosine)
    sin_rows = spread(pick_ref[0, 1], sine)
    upper = mask_ref[0][:, :1] > 0
    value = now[...]
    value = jnp.where(upper, permuted(value, order, False), value)
    now[...] = value
    for index, bit in enumerate(bits):

        @pl.when(step == index)
        def _():
            kept_ref[0] = cos_rows * now[...] + sin_rows * swap_groups(now[...], each << bit)

    value = kept_ref[0]
    value = jnp.where(upper, permuted(value, order, True), value)
    now[...] = value

    @pl.when(step == len(bits) - 1)
    def _():
        z_ref[...] = value.astype(BF16)


def backward_kernel(bits, each, g_ref, kept_ref, cos_ref, sin_ref, order_ref, pick_ref, sum_ref,
                    mask_ref, low_ref, up_ref, now, other, pair):
    step = pl.program_id(0)

    @pl.when(step == 0)
    def _():
        now[...] = g_ref[...].astype(F32)

    order = order_ref[0]
    cos_rows = spread(pick_ref[0, 0], cos_ref[0])
    sin_rows = spread(pick_ref[0, 1], sin_ref[0])
    upper = mask_ref[0][:, :1] > 0
    value = now[...]
    value = jnp.where(upper, permuted(value, order, False), value)
    now[...] = value
    for index, bit in enumerate(reversed(bits)):

        @pl.when(step == index)
        def _():
            other[...] = swap_groups(now[...], each << bit)
            pair[...] = swap_groups(kept_ref[0], each << bit)

    value = now[...]
    partner = other[...]
    terms = partner * kept_ref[0] - value * pair[...]
    sums = spread(sum_ref[0], terms)
    low_ref[0] = sums
    before = cos_rows * value - sin_rows * partner
    rows = value.shape[0]
    back = permuted(jnp.concatenate([before, sums], axis=0), order, True)
    up_ref[0] = back[rows:]
    now[...] = jnp.where(upper, back[:rows], before)


def tables(bits, groups, each):
    sections, rows = len(bits), groups * each
    pick = np.zeros((sections, 2, rows, groups // 2), np.float32)
    total = np.zeros((sections, groups // 2, rows), np.float32)
    mask = np.zeros((sections, rows, 128), np.float32)
    for s, bit in enumerate(bits):
        stride = 1 << bit
        for row in range(rows):
            group = row // each
            is_upper = group // stride % 2
            pair = group // (2 * stride) * stride + group % stride
            pick[s, 0, row, pair] = 1
            pick[s, 1, row, pair] = 1 if is_upper else -1
            mask[s, row] = is_upper
            if not is_upper:
                total[s, pair, row] = 1
    return pick, total, mask


def block(shape, index=lambda s: s):
    rest = (0,) * (len(shape) - 1)
    return pl.BlockSpec(shape, lambda s: (index(s),) + rest)


def whole(shape):
    return pl.BlockSpec(shape, lambda s: (0,) * len(shape))


def turn_forward(bits, each, x, low, up, order, pick, mask):
    sections, width = order.shape[0], order.shape[1]
    rows, pairs = x.shape[0], low.shape[1]
    return pl.pallas_call(
        functools.partial(forward_kernel, bits, each),
        grid=(sections,),
        in_specs=[
            whole((rows, width)),
            block((1, pairs, width)),
            block((1, pairs, width)),
            block((1, width, width)),
            block((1, 2, rows, pairs)),
            block((1, rows, 128)),
        ],
        out_specs=[
            whole((rows, width)),
            block((1, rows, width)),
            block((1, pairs, width)),
            block((1, pairs, width)),
        ],
        out_shape=[
            jax.ShapeDtypeStruct((rows, width), BF16),
            jax.ShapeDtypeStruct((sections, rows, width), F32),
            jax.ShapeDtypeStruct((sections, pairs, width), F32),
            jax.ShapeDtypeStruct((sections, pairs, width), F32),
        ],
        scratch_shapes=[pltpu.VMEM((rows, width), F32)],
        compiler_params=pltpu.CompilerParams(vmem_limit_bytes=32 << 20),
        cost_estimate=pl.CostEstimate(
            flops=sections * 10 * rows * width * width, bytes_accessed=12 << 20, transcendentals=0
        ),
        name="turn_forward",
    )(x, low, up, order, pick, mask)


def turn_backward(bits, each, g, kept, cosine, sine, order, pick, total, mask):
    sections, width = order.shape[0], order.shape[1]
    rows, pairs = g.shape[0], cosine.shape[1]
    last = sections - 1

    def flip(s):
        return last - s

    return pl.pallas_call(
        functools.partial(backward_kernel, bits, each),
        grid=(sections,),
        in_specs=[
            whole((rows, width)),
            block((1, rows, width), flip),
            block((1, pairs, width), flip),
            block((1, pairs, width), flip),
            block((1, width, width), flip),
            block((1, 2, rows, pairs), flip),
            block((1, pairs, rows), flip),
            block((1, rows, 128), flip),
        ],
        out_specs=[block((1, pairs, width), flip), block((1, pairs, width), flip)],
        out_shape=[jax.ShapeDtypeStruct((sections, pairs, width), F32)] * 2,
        scratch_shapes=[pltpu.VMEM((rows, width), F32)] * 3,
        compiler_params=pltpu.CompilerParams(vmem_limit_bytes=32 << 20),
        cost_estimate=pl.CostEstimate(
            flops=sections * 10 * rows * width * width, bytes_accessed=12 << 20, transcendentals=0
        ),
        name="turn_backward",
    )(g, kept, cosine, sine, order, pick, total, mask)


def split_pairs(values, bit):
    stride = 1 << bit
    shaped = values.reshape((-1, 2, stride) + values.shape[1:])
    return (
        shaped[:, 0].reshape((-1,) + values.shape[1:]),
        shaped[:, 1].reshape((-1,) + values.shape[1:]),
    )


def join_pairs(low, up, bit):
    stride = 1 << bit
    shape = low.shape[1:]
    both = jnp.stack([low.reshape((-1, stride) + shape), up.reshape((-1, stride) + shape)], axis=1)
    return both.reshape((-1,) + shape)


def scale_up(value):
    top = jnp.max(jnp.abs(value))
    scale = jnp.float32(1)
    exponent = jnp.float32(0)
    for step in STEPS:
        fits = top * scale * jnp.float32(2.0**step) < 2.0**15
        scale = jnp.where(fits, scale * jnp.float32(2.0**step), scale)
        exponent = jnp.where(fits, exponent + step, exponent)
    return scale, exponent


def scale_down(exponent):
    scale = jnp.ones_like(exponent)
    for step in STEPS:
        takes = exponent >= step
        scale = jnp.where(takes, scale * jnp.float32(2.0**-step), scale)
        exponent = jnp.where(takes, exponent - step, exponent)
    return scale


def per_device(tokens, up_weight, angles, pair_order, cotangent):
    groups = lax.axis_size(TENSOR)
    near = lax.axis_size(NEAR)
    depth = lax.axis_size(Z)
    sides = lax.axis_size("xh")
    width = up_weight.shape[1]
    hidden = up_weight.shape[0]
    sections = pair_order.shape[0]
    bit_count = groups.bit_length() - 1
    bits = [(bit_count - 1 - s) % bit_count for s in range(sections)]
    core = lax.axis_index("c")
    other_core = [(0, 1), (1, 0)]
    rows = cotangent.shape[0]
    own_rows = tokens.shape[0] // groups
    each = sides * own_rows
    pick, total, mask = tables(bits, groups, each)

    mine = cotangent.reshape(sides, groups, own_rows, hidden).transpose(1, 0, 2, 3)
    mine = mine.reshape(1, rows, hidden)
    cot_own = all_to_all(jnp.broadcast_to(mine, (near, rows, hidden)), NEAR)
    cot_other = lax.ppermute(cot_own, "c", other_core)

    def gradient_part(cot):
        return jnp.dot(
            cot.reshape(near * rows, hidden), up_weight, preferred_element_type=F32
        ).astype(BF16).reshape(near, rows, width)

    part_own = gradient_part(cot_own)
    part_other = gradient_part(cot_other)
    is_first = core == 0
    part = jnp.stack(
        [jnp.where(is_first, part_own, part_other), jnp.where(is_first, part_other, part_own)],
        axis=1,
    )
    gradient = lax.psum_scatter(
        part.reshape(depth * rows, width), Z, scatter_dimension=0, tiled=True
    )

    spread_tokens = jnp.broadcast_to(
        tokens.reshape(1, groups, own_rows, width), (sides, groups, own_rows, width)
    ).reshape(sides * groups, own_rows, width)
    got = all_to_all(spread_tokens, PLANE).reshape(sides, groups, own_rows, width)
    x = got.transpose(1, 0, 2, 3).reshape(groups * each, width)
    all_angles = all_to_all(
        jnp.broadcast_to(angles.reshape(1, sections * width), (groups, sections * width)), TENSOR
    ).reshape(groups, sections, width)
    pairs = [split_pairs(all_angles[:, s], bits[s]) for s in range(sections)]
    low = jnp.stack([p[0] for p in pairs])
    up = jnp.stack([p[1] for p in pairs])
    order = (
        lax.broadcasted_iota(jnp.int32, (sections, width, width), 1) == pair_order[:, None, :]
    ).astype(BF16)
    pick = jnp.asarray(pick, BF16)
    total = jnp.asarray(total, BF16)
    mask = jnp.asarray(mask)
    rotated, kept, cosine, sine = turn_forward(bits, each, x, low, up, order, pick, mask)

    back = all_to_all(rotated.reshape(groups, each, width), TENSOR).reshape(rows, width)
    back = back.astype(F32)
    scale, exponent = scale_up(back)
    packed = jnp.concatenate(
        [(back * scale).astype(jnp.float16), jnp.full((rows, 128), exponent, jnp.float16)], axis=1
    )
    token_all = lax.all_gather(packed, Z, axis=0, tiled=True)
    shrink = scale_down(token_all[:, width].astype(F32)).reshape(near, 2, rows, 1)
    token_all = token_all[:, :width].astype(BF16).reshape(near, 2, rows, width)

    def projected_part(which):
        chosen = lax.dynamic_index_in_dim(token_all, which, 1, keepdims=False)
        factor = lax.dynamic_index_in_dim(shrink, which, 1, keepdims=False)
        return factor * lax.dot_general(
            chosen, up_weight, (((2,), (1,)), ((), ())), preferred_element_type=F32
        )

    sent = lax.ppermute(projected_part(1 - core).astype(BF16), "c", other_core)
    both = (projected_part(core).astype(BF16).astype(F32) + sent.astype(F32)).astype(BF16)
    terms = all_to_all(both, NEAR).astype(F32)
    projected = jnp.sum(terms, axis=0).astype(BF16)
    projected = projected.reshape(groups, sides, own_rows, hidden).transpose(1, 0, 2, 3)
    projected = projected.reshape(rows, hidden)

    g = all_to_all(gradient.reshape(groups, each, width), TENSOR).reshape(groups * each, width)
    low_sums, up_sums = turn_backward(
        bits, each, g, kept, cosine, sine, order, pick, total, mask
    )
    sums = jnp.stack(
        [join_pairs(low_sums[s], up_sums[s], bits[s]) for s in range(sections)], axis=1
    ).reshape(1, groups, sections * width)
    sums = jnp.broadcast_to(sums, (sides, groups, sections * width))
    sums = all_to_all(sums.reshape(sides * groups, sections * width), PLANE)
    sums = jnp.sum(sums, axis=0, keepdims=True)
    sums = all_to_all(jnp.broadcast_to(sums, (depth, sections * width)), Z)
    angle_grads = jnp.sum(sums, axis=0).reshape(sections, width)
    return projected, angle_grads


def solution(mesh):
    fine = jax.sharding.Mesh(
        mesh.devices.reshape(16, 2, 2, 4, 2), ("z", "xh", "xl", "y", "c")
    )
    dp, tensor = ("z", "xh"), TENSOR
    placed = (P(dp, tensor), P(dp, tensor), P(None, tensor), P(), P(tensor, dp))
    return jax.shard_map(
        per_device,
        mesh=fine,
        in_specs=placed,
        out_specs=(P(tensor, dp), P(None, tensor)),
        check_vma=False,
    )
```

time: 1170 us -> 250 us (0.21)
  waiting for transfers between devices: 826 us -> 53.2 us
  local copies, waits for them, and re-layouts: 106 us -> 20.1 us
  blocking collectives: 144 us -> 59.4 us
  starting transfers between devices: 37.5 us -> 56.7 us
  other arithmetic: 30.4 us -> 14.3 us
  Pallas kernels: 0 us -> 13.8 us
    reduce_scatter x2 -> x1, waiting for transfers between devices: 651 us -> 0.01 us  [per_device(): lax.psum_scatter(part.reshape(depth * rows, width), Z, scatter_dimension=...]
    all_gather x2 -> x0, waiting for transfers between devices: 158 us -> none  [the longest x1 148 us: per_device(): token_all = lax.all_gather(rotated, 'dp', axis=0, tiled=True)]
    psum x1 -> x0, blocking collectives: 144 us -> none  [per_device(): angle_grads = lax.psum(own_sums, 'dp')]
    gather x38 -> x0, local copies, waits for them, and re-layouts: 98.8 us -> none  [the longest x8 19.7 us: per_device(): jnp.take(new_partner, inverses[factor], axis=-1)]
    all_gather x0 -> x1, blocking collectives: none -> 59.4 us  [per_device(): token_all = lax.all_gather(packed, Z, axis=0, tiled=True)]
    all_to_all x0 -> x8, waiting for transfers between devices: none -> 53.2 us  [all_to_all(): return lax.all_to_all(array, axes, 0, 0, tiled=True)]
    all_to_all x0 -> x8, starting transfers between devices: none -> 52.6 us  [all_to_all(): return lax.all_to_all(array, axes, 0, 0, tiled=True)]
    ppermute x12 -> x2, starting transfers between devices: 37.4 us -> 4.1 us  [the longest x1 2.06 us: per_device(): cot_other = lax.ppermute(cot_own, 'c', other_core)]
  transfers between devices with their start and end apart: 16 -> 11, of which waited for: 9 -> 6; matrix products, arithmetic and copies ran while one was open for 8% -> 11% of each run, Pallas kernels for 0% -> 6%
where the time goes in v1:
time: 250 us; the launch traced here: 248 us
  blocking collectives  59.4 us (24%)
  starting transfers between devices  56.7 us (23%)
  waiting for transfers between devices  53.2 us (21%)
  local copies, waits for them, and re-layouts  20.1 us (8%)
  between operations  18.5 us (7%)
  other arithmetic  14.3 us (6%)
  Pallas kernels  13.8 us (6%)
  matrix products  12.1 us (5%)
    all_gather x1, blocking collectives, per_device(): token_all = lax.all_gather(packed, Z, axis=0, tiled=True)  59.4 us
    all_to_all x8, waiting for transfers between devices, all_to_all(): return lax.all_to_all(array, axes, 0, 0, tiled=True)  53.2 us
    all_to_all x8, starting transfers between devices, all_to_all(): return lax.all_to_all(array, axes, 0, 0, tiled=True)  52.6 us
    unnamed x22, local copies, waits for them, and re-layouts  8.45 us
    pallas_call x1, Pallas kernels, turn_forward(): pl.pallas_call(functools.partial(forward_kernel, bits, each), grid=(secti...  7.5 us
    dot_general x2, matrix products, projected_part(): lax.dot_general(chosen, up_weight, (((2,), (1,)), ((), ())), preferred_el...  7.19 us
    convert_element_type x1, other arithmetic, per_device(): order = (lax.broadcasted_iota(jnp.int32, (sections, width, width), 1) ==...  6.83 us
    pallas_call x1, Pallas kernels, turn_backward(): pl.pallas_call(functools.partial(backward_kernel, bits, each), grid=(sect...  6.29 us
  transfers between devices with their start and end apart: 11, of which 6 were waited for; matrix products, arithmetic and copies ran while one was open for 11% of the time, Pallas kernels for 6%

profile of v1, /device:TPU:24, one launch (start us, length us, event | category | flops | bytes accessed | tf_op | source)
XLA Modules:
  0.0 248.1 jit_solution(3093918209523033381)
XLA Ops:
  7.2 0.0 copy-start
  7.2 1.1 reshape.225
  8.3 0.1 copy.101
  8.4 0.0 copy-start.9
  8.4 0.1 broadcast_in_dim.44
  8.5 1.0 broadcast_in_dim.45
  9.5 9.8 %all-to-all-start.4 = ((bf16[8,64,832]{2,1,0:T(8,128)(2,1)}), bf16[8,64,832]{2,1,0:T(8,128)(2,1)}, u32[]{:S(2)}, u32[]{:S(2)}) async-start(bf16[8,64,832]{2,1,0:T(8,128)(2,1)} %broadcast_in_dim.45), calls=%async_computation.4 | async-start | bytes 1835008 | tf_op jit(solution)/shard_map/all_to_all | solution.py:21
  19.4 8.5 %all-to-all-done.4 = bf16[8,64,832]{2,1,0:T(8,128)(2,1)} async-done(((bf16[8,64,832]{2,1,0:T(8,128)(2,1)}), bf16[8,64,832]{2,1,0:T(8,128)(2,1)}, u32[]{:S(2)}, u32[]{:S(2)}) %all-to-all-start.4) | async-done | bytes 852000 | tf_op jit(solution)/shard_map/all_to_all | solution.py:21
  27.9 0.7 broadcast_in_dim.40
  28.6 6.3 %all-to-all-start = ((bf16[32,2,1024]{2,1,0:T(2,128)(2,1)}), bf16[32,2,1024]{2,1,0:T(2,128)(2,1)S(1)}, u32[]{:S(2)}, u32[]{:S(2)}) async-start(bf16[32,2,1024]{2,1,0:T(2,128)(2,1)} %bitcast), calls=%async_computation | async-start | bytes 262144 | tf_op jit(solution)/shard_map/all_to_all | solution.py:21
  34.9 2.1 collective-permute-start.1
  37.0 4.0 %all-to-all-done = bf16[32,2,1024]{2,1,0:T(2,128)(2,1)S(1)} async-done(((bf16[32,2,1024]{2,1,0:T(2,128)(2,1)}), bf16[32,2,1024]{2,1,0:T(2,128)(2,1)S(1)}, u32[]{:S(2)}, u32[]{:S(2)}) %all-to-all-start) | async-done | bytes 131104 | tf_op jit(solution)/shard_map/all_to_all | solution.py:21
  41.0 0.9 broadcast_in_dim.42
  41.9 5.4 %all-to-all-start.1 = ((f32[16,1,4096]{2,1,0:T(1,128)}), f32[16,1,4096]{2,1,0:T(1,128)S(1)}, u32[]{:S(2)}, u32[]{:S(2)}) async-start(f32[16,1,4096]{2,1,0:T(1,128)} %broadcast_in_dim.42), calls=%async_computation.1 | async-start | bytes 524288 | tf_op jit(solution)/shard_map/all_to_all | solution.py:21
  47.3 0.0 reduce-scatter.2.cloned.1.call-start
  47.3 6.8 %fusion.order_ref = bf16[4,1024,1024]{2,1,0:T(8,128)(2,1)} fusion(s32[4,1024]{1,0:T(4,128)S(1)} %copy-done.8), kind=kLoop, calls=%fused_computation.1 | loop fusion | flops 8388608 | bytes 8404992 | tf_op jit(solution)/shard_map/convert_element_type | solution.py:308
  54.2 0.1 copy.73
  54.3 0.1 reshape.219.x_ref
  54.4 0.0 all-to-all-done.1
  54.4 0.6 reduce.4
  55.0 0.2 reshape.220
  55.2 2.4 convolution_convert_fusion.1
  57.7 0.0 collective-permute-done.1
  57.7 2.4 broadcast_select_fusion.1
  60.1 1.5 pad_maximum_fusion
  61.6 0.0 reduce-scatter.2.cloned.1.call-update
  61.7 0.4 fusion.19
  62.4 0.1 copy-done.3
  62.5 0.1 copy-done.4
  62.6 3.4 %copy-done.1 = bf16[4,1024,1024]{2,1,0:T(8,128)(2,1)S(1)} copy-done((bf16[4,1024,1024]{2,1,0:T(8,128)(2,1)S(1)}, bf16[4,1024,1024]{2,1,0:T(8,128)(2,1)}, u32[]{:S(2)}) %copy-start.1) | copy-done | bytes 8388632
  66.0 7.5 %turn_forward.1 = (bf16[64,1024]{1,0:T(8,128)(2,1)S(1)}, f32[4,64,1024]{2,1,0:T(8,128)S(1)}, f32[4,8,1024]{2,1,0:T(8,128)S(1)}, f32[4,8,1024]{2,1,0:T(8,128)S(1)}) custom-call(bf16[64,1024]{1,0:T(8,128)(2,1)S(1)} %reshape.219.x_ref, f32[4,8,1024]{2,1,0:T(8,128)S(1)} %pad_maximum_fusion.1.low_ref, f32[4,8,1024]{2,1,0:T(8,128)S(1)} %pad_maximum_fusion.2.up_ref, ...), custom_call_target="tpu_custom_call" | custom-call | flops 2684354560 | bytes 12582912 | tf_op jit(solution)/shard_map/turn_forward/pallas_call | solution.py:157
  73.5 0.7 reshape.221
  74.2 5.8 %all-to-all-start.2 = ((bf16[16,4,1024]{2,1,0:T(4,128)(2,1)}), bf16[16,4,1024]{2,1,0:T(4,128)(2,1)S(1)}, u32[]{:S(2)}, u32[]{:S(2)}) async-start(bf16[16,4,1024]{2,1,0:T(4,128)(2,1)} %reshape.221), calls=%async_computation.2 | async-start | bytes 262144 | tf_op jit(solution)/shard_map/all_to_all | solution.py:21
  80.0 4.6 %all-to-all-done.2 = bf16[16,4,1024]{2,1,0:T(4,128)(2,1)S(1)} async-done(((bf16[16,4,1024]{2,1,0:T(4,128)(2,1)}), bf16[16,4,1024]{2,1,0:T(4,128)(2,1)S(1)}, u32[]{:S(2)}, u32[]{:S(2)}) %all-to-all-start.2) | async-done | bytes 131104 | tf_op jit(solution)/shard_map/all_to_all | solution.py:21
  84.6 0.7 fusion.15
  89.2 0.1 fusion.16
  89.4 59.4 %all-gather.1 = f16[1024,1152]{1,0:T(8,128)(2,1)S(1)} all-gather(f16[64,1152]{1,0:T(8,128)(2,1)S(1)} %concatenate.3), channel_id=1, replica_groups=mesh['z'=16,'xh'=2,'xl'=2,'y'=4,'c'=2] {'z'}, dimensions={0}, use_global_device_ids=true | all-gather | bytes 2506752 | tf_op jit(solution)/shard_map/all_gather | solution.py:320
  148.8 1.5 copy-done.6
  150.3 0.2 convert_reduce_fusion
  150.5 0.1 reshape.232
  150.7 3.5 %slice_convert_fusion = bf16[1024,1024]{1,0:T(8,128)(2,1)} fusion(f16[1024,1152]{1,0:T(8,128)(2,1)} %copy-done.6), kind=kLoop, calls=%fused_computation.2 | loop fusion | flops 1048576 | bytes 4194304 | tf_op jit(solution)/shard_map/convert_element_type | solution.py:322
  154.2 1.6 reshape.229
  155.8 5.0 %all-to-all-start.5 = ((bf16[16,4,1024]{2,1,0:T(4,128)(2,1)}), bf16[16,4,1024]{2,1,0:T(4,128)(2,1)S(1)}, u32[]{:S(2)}, u32[]{:S(2)}) async-start(bf16[16,4,1024]{2,1,0:T(4,128)(2,1)} %reshape.229), calls=%async_computation.6 | async-start | bytes 262144 | tf_op jit(solution)/shard_map/all_to_all | solution.py:21
  160.8 3.5 %multiply_convert_fusion = bf16[8,64,832]{2,1,0:T(8,128)(2,1)} fusion(bf16[832,1024]{1,0:T(8,128)(2,1)S(1)} %copy-done, bf16[8,2,64,1024]{3,2,1,0:T(8,128)(2,1)} %bitcast.76, s32[]{:T(128)S(6)} %select_n.214, f32[8,64]{1,0:T(8,128)S(1)} %bitcast.94), kind=kOutput, calls=%fused_computation.5 | convolution fusion | flops 873267200 | bytes 3606532 | tf_op jit(solution)/shard_map/dot_general | solution.py:327
  164.3 2.0 collective-permute-start
  166.3 0.0 all-to-all-done.5
  166.4 3.4 %copy-done.2 = bf16[4,1024,1024]{2,1,0:T(8,128)(2,1)S(1)} copy-done((bf16[4,1024,1024]{2,1,0:T(8,128)(2,1)S(1)}, bf16[4,1024,1024]{2,1,0:T(8,128)(2,1)}, u32[]{:S(2)}) %copy-start.2) | copy-done | bytes 8388632
  169.8 6.3 %turn_backward.1 = (f32[4,8,1024]{2,1,0:T(8,128)S(1)}, f32[4,8,1024]{2,1,0:T(8,128)S(1)}) custom-call(bf16[64,1024]{1,0:T(8,128)(2,1)S(1)} %reshape.230.g_ref, f32[4,64,1024]{2,1,0:T(8,128)S(1)} %get-tuple-element.9.kept_ref, f32[4,8,1024]{2,1,0:T(8,128)S(1)} %get-tuple-element.10.cos_ref, f32[4,8,1024]{2,1,0:T(8,128)S(1)} %get-tuple-element.11.sin_ref, ...), custom_call_target="tpu_custom_call" | custom-call | flops 2684354560 | bytes 12582912 | tf_op jit(solution)/shard_map/turn_backward/pallas_call | solution.py:197
  176.2 0.1 copy.84
  176.6 1.4 all_to_all.35
  178.0 6.3 %all-to-all-start.6 = ((f32[32,1,4096]{2,1,0:T(1,128)}), f32[32,1,4096]{2,1,0:T(1,128)S(1)}, u32[]{:S(2)}, u32[]{:S(2)}) async-start(f32[32,1,4096]{2,1,0:T(1,128)} %all_to_all.35), calls=%async_computation.7 | async-start | bytes 1048576 | tf_op jit(solution)/shard_map/all_to_all | solution.py:21
  184.3 3.7 %add_convert_fusion = bf16[8,64,832]{2,1,0:T(8,128)(2,1)} fusion(bf16[8,64,832]{2,1,0:T(8,128)(2,1)} %collective-permute-done, bf16[832,1024]{1,0:T(8,128)(2,1)S(1)} %copy-done, bf16[8,2,64,1024]{3,2,1,0:T(8,128)(2,1)} %bitcast.77, s32[]{:T(128)S(6)} %select_n.213, f32[8,64]{1,0:T(8,128)S(1)} %bitcast.93), kind=kOutput, calls=%fused_computation.4 | convolution fusion | flops 874971136 | bytes 4524036 | tf_op jit(solution)/shard_map/dot_general | solution.py:327
  188.0 6.0 %all-to-all-done.6 = f32[32,1,4096]{2,1,0:T(1,128)S(1)} async-done(((f32[32,1,4096]{2,1,0:T(1,128)}), f32[32,1,4096]{2,1,0:T(1,128)S(1)}, u32[]{:S(2)}, u32[]{:S(2)}) %all-to-all-start.6) | async-done | bytes 524320 | tf_op jit(solution)/shard_map/all_to_all | solution.py:21
  194.0 5.2 %all-to-all-start.3 = ((bf16[8,64,832]{2,1,0:T(8,128)(2,1)}), bf16[8,64,832]{2,1,0:T(8,128)(2,1)S(1)}, u32[]{:S(2)}, u32[]{:S(2)}) async-start(bf16[8,64,832]{2,1,0:T(8,128)(2,1)} %add_convert_fusion), calls=%async_computation.3 | async-start | bytes 1835008 | tf_op jit(solution)/shard_map/all_to_all | solution.py:21
  199.2 0.4 reduce_sum.31
  199.5 12.9 %all-to-all-done.3 = bf16[8,64,832]{2,1,0:T(8,128)(2,1)S(1)} async-done(((bf16[8,64,832]{2,1,0:T(8,128)(2,1)}), bf16[8,64,832]{2,1,0:T(8,128)(2,1)S(1)}, u32[]{:S(2)}, u32[]{:S(2)}) %all-to-all-start.3) | async-done | bytes 852000 | tf_op jit(solution)/shard_map/all_to_all | solution.py:21
  212.4 0.9 broadcast_in_dim.48
  213.3 8.9 %all-to-all-start.7 = ((f32[16,1,4096]{2,1,0:T(1,128)}), f32[16,1,4096]{2,1,0:T(1,128)S(1)}, u32[]{:S(2)}, u32[]{:S(2)}) async-start(f32[16,1,4096]{2,1,0:T(1,128)} %broadcast_in_dim.48), calls=%async_computation.8 | async-start | bytes 524288 | tf_op jit(solution)/shard_map/all_to_all | solution.py:21
  222.2 0.1 reduce_sum.30
  222.4 0.1 copy.76
  222.5 0.7 reshape.224
  223.2 17.2 %all-to-all-done.7 = f32[16,1,4096]{2,1,0:T(1,128)S(1)} async-done(((f32[16,1,4096]{2,1,0:T(1,128)}), f32[16,1,4096]{2,1,0:T(1,128)S(1)}, u32[]{:S(2)}, u32[]{:S(2)}) %all-to-all-start.7) | async-done | bytes 262176 | tf_op jit(solution)/shard_map/all_to_all | solution.py:21
  240.5 0.2 reduce_sum.32
  240.6 0.6 reshape.231
  (54 shorter events, 0.9 us)
Async XLA Ops:
  7.2 48.1 %copy-start = (bf16[832,1024]{1,0:T(8,128)(2,1)S(1)}, bf16[832,1024]{1,0:T(8,128)(2,1)}, u32[]{:S(2)}) copy-start(bf16[832,1024]{1,0:T(8,128)(2,1)} %param.9) | copy-start | bytes 5111812
  7.2 12.2 %copy-start.7 = (bf16[32,1024]{1,0:T(8,128)(2,1)S(1)}, bf16[32,1024]{1,0:T(8,128)(2,1)}, u32[]{:S(2)}) copy-start(bf16[32,1024]{1,0:T(8,128)(2,1)} %param.8) | copy-start | bytes 196612
  8.4 26.5 %copy-start.9 = (f32[4,1024]{1,0:T(4,128)S(1)}, f32[4,1024]{1,0:T(4,128)}, u32[]{:S(2)}) copy-start(f32[4,1024]{1,0:T(4,128)} %param.10) | copy-start | bytes 49156
  9.5 37.8 %copy-start.8 = (s32[4,1024]{1,0:T(4,128)S(1)}, s32[4,1024]{1,0:T(4,128)}, u32[]{:S(2)}) copy-start(s32[4,1024]{1,0:T(4,128)} %param.11) | copy-start | bytes 49156
  9.5 18.4 %all-to-all-start.4 = ((bf16[8,64,832]{2,1,0:T(8,128)(2,1)}), bf16[8,64,832]{2,1,0:T(8,128)(2,1)}, u32[]{:S(2)}, u32[]{:S(2)}) async-start(bf16[8,64,832]{2,1,0:T(8,128)(2,1)} %broadcast_in_dim.45), calls=%async_computation.4 | async-start | bytes 1835008 | tf_op jit(solution)/shard_map/all_to_all | solution.py:21
  28.6 12.3 %all-to-all-start = ((bf16[32,2,1024]{2,1,0:T(2,128)(2,1)}), bf16[32,2,1024]{2,1,0:T(2,128)(2,1)S(1)}, u32[]{:S(2)}, u32[]{:S(2)}) async-start(bf16[32,2,1024]{2,1,0:T(2,128)(2,1)} %bitcast), calls=%async_computation | async-start | bytes 262144 | tf_op jit(solution)/shard_map/all_to_all | solution.py:21
  34.9 22.7 %collective-permute-start.1 = (bf16[8,64,832]{2,1,0:T(8,128)(2,1)}, bf16[8,64,832]{2,1,0:T(8,128)(2,1)}, u32[]{:S(2)}, u32[]{:S(2)}) collective-permute-start(bf16[8,64,832]{2,1,0:T(8,128)(2,1)} %all-to-all-done.4), channel_id=1, source_target_pairs={{0,1},{1,0},{2,3},{3,2},{4,5},{5,4},{6,7},{7,6},{8,9},{9,8},{10,11... | collective-permute-start | bytes 2555912 | tf_op jit(solution)/shard_map/ppermute | solution.py:277
  41.9 12.5 %all-to-all-start.1 = ((f32[16,1,4096]{2,1,0:T(1,128)}), f32[16,1,4096]{2,1,0:T(1,128)S(1)}, u32[]{:S(2)}, u32[]{:S(2)}) async-start(f32[16,1,4096]{2,1,0:T(1,128)} %broadcast_in_dim.42), calls=%async_computation.1 | async-start | bytes 524288 | tf_op jit(solution)/shard_map/all_to_all | solution.py:21
  47.3 106.9 %reduce-scatter.2.cloned.1.call-start = ((), (), s32[]{:S(2)}) async-start(), calls=%async_computation.9 | async-start | bytes 2228224 | tf_op jit(solution)/shard_map/reduce_scatter | solution.py:291
  61.6 0.9 copy-start.3
  61.6 1.0 copy-start.4
  62.6 3.4 %copy-start.1 = (bf16[4,1024,1024]{2,1,0:T(8,128)(2,1)S(1)}, bf16[4,1024,1024]{2,1,0:T(8,128)(2,1)}, u32[]{:S(2)}) copy-start(bf16[4,1024,1024]{2,1,0:T(8,128)(2,1)} %fusion.order_ref) | copy-start | bytes 25165828
  74.2 10.4 %all-to-all-start.2 = ((bf16[16,4,1024]{2,1,0:T(4,128)(2,1)}), bf16[16,4,1024]{2,1,0:T(4,128)(2,1)S(1)}, u32[]{:S(2)}, u32[]{:S(2)}) async-start(bf16[16,4,1024]{2,1,0:T(4,128)(2,1)} %reshape.221), calls=%async_computation.2 | async-start | bytes 262144 | tf_op jit(solution)/shard_map/all_to_all | solution.py:21
  148.8 1.5 copy-start.6
  155.8 10.5 %all-to-all-start.5 = ((bf16[16,4,1024]{2,1,0:T(4,128)(2,1)}), bf16[16,4,1024]{2,1,0:T(4,128)(2,1)S(1)}, u32[]{:S(2)}, u32[]{:S(2)}) async-start(bf16[16,4,1024]{2,1,0:T(4,128)(2,1)} %reshape.229), calls=%async_computation.6 | async-start | bytes 262144 | tf_op jit(solution)/shard_map/all_to_all | solution.py:21
  160.8 5.6 %copy-start.5 = (bf16[4,8,64]{2,1,0:T(8,128)(2,1)S(1)}, bf16[4,8,64]{2,1,0:T(8,128)(2,1)}, u32[]{:S(2)}) copy-start(bf16[4,8,64]{2,1,0:T(8,128)(2,1)} %constant.89.clone.sum_ref) | copy-start | bytes 12292
  164.3 20.0 %collective-permute-start = (bf16[8,64,832]{2,1,0:T(8,128)(2,1)}, bf16[8,64,832]{2,1,0:T(8,128)(2,1)}, u32[]{:S(2)}, u32[]{:S(2)}) collective-permute-start(bf16[8,64,832]{2,1,0:T(8,128)(2,1)} %multiply_convert_fusion), channel_id=1, source_target_pairs={{0,1},{1,0},{2,3},{3,2},{4,5},{5,4},{6,7},{7,6},{8,9},{9,8},{10,11... | collective-permute-start | bytes 2555912 | tf_op jit(solution)/shard_map/ppermute | solution.py:331
  166.4 3.4 %copy-start.2 = (bf16[4,1024,1024]{2,1,0:T(8,128)(2,1)S(1)}, bf16[4,1024,1024]{2,1,0:T(8,128)(2,1)}, u32[]{:S(2)}) copy-start(bf16[4,1024,1024]{2,1,0:T(8,128)(2,1)} %fusion.order_ref) | copy-start | bytes 25165828
  178.0 16.0 %all-to-all-start.6 = ((f32[32,1,4096]{2,1,0:T(1,128)}), f32[32,1,4096]{2,1,0:T(1,128)S(1)}, u32[]{:S(2)}, u32[]{:S(2)}) async-start(f32[32,1,4096]{2,1,0:T(1,128)} %all_to_all.35), calls=%async_computation.7 | async-start | bytes 1048576 | tf_op jit(solution)/shard_map/all_to_all | solution.py:21
  194.0 18.4 %all-to-all-start.3 = ((bf16[8,64,832]{2,1,0:T(8,128)(2,1)}), bf16[8,64,832]{2,1,0:T(8,128)(2,1)S(1)}, u32[]{:S(2)}, u32[]{:S(2)}) async-start(bf16[8,64,832]{2,1,0:T(8,128)(2,1)} %add_convert_fusion), calls=%async_computation.3 | async-start | bytes 1835008 | tf_op jit(solution)/shard_map/all_to_all | solution.py:21
  213.3 27.1 %all-to-all-start.7 = ((f32[16,1,4096]{2,1,0:T(1,128)}), f32[16,1,4096]{2,1,0:T(1,128)S(1)}, u32[]{:S(2)}, u32[]{:S(2)}) async-start(f32[16,1,4096]{2,1,0:T(1,128)} %broadcast_in_dim.48), calls=%async_computation.8 | async-start | bytes 524288 | tf_op jit(solution)/shard_map/all_to_all | solution.py:21
Sparse Core Ops, SparseCore 0:
  61.8 79.3 reduce-scatter.1

commit v2 on v0

v2 whole, which is shorter than its diff:
```python
import functools

import jax
import jax.numpy as jnp
from jax import lax
from jax.experimental import pallas as pl
from jax.experimental.pallas import tpu as pltpu
from jax.sharding import PartitionSpec as P

BF16 = jnp.bfloat16
F16 = jnp.float16
F32 = jnp.float32
Z = "z"
TENSOR = ("xl", "y", "c")
NEAR = ("xl", "y")
PLANE = ("xh", "xl", "y", "c")
STEPS = (64, 32, 16, 8, 4, 2)
LANES = 128
VMEM = 24 << 20


def all_to_all(array, axes):
    return lax.all_to_all(array, axes, 0, 0, tiled=True)


def copies(array, count):
    return jnp.broadcast_to(array[None], (count,) + array.shape).reshape(
        (count * array.shape[0],) + array.shape[1:]
    )


def product(left, right, transposed):
    dims = (((1,), (1 if transposed else 0,)), ((), ()))
    return lax.dot_general(left, right, dims, preferred_element_type=F32)


def permuted(value, matrix, transposed):
    rows = value.shape[0]
    high = value.astype(BF16)
    low = (value - high.astype(F32)).astype(BF16)
    out = product(jnp.concatenate([high, low], axis=0), matrix, transposed)
    return out[:rows] + out[rows:]


def one_hot(order_row):
    width = order_row.shape[1]
    rows = lax.broadcasted_iota(jnp.int32, (width, width), 0)
    return jnp.where(rows == order_row, 1.0, 0.0).astype(BF16)


def upper_rows(rows, groups, stride):
    group = lax.broadcasted_iota(jnp.int32, (rows, 1), 0) & (groups - 1)
    return (group & stride) != 0


def swap_rows(value, distance):
    rows = value.shape[0]
    if distance >= 8:
        parts = []
        for i in range(0, rows, 2 * distance):
            parts += [value[i + distance : i + 2 * distance], value[i : i + distance]]
        return jnp.concatenate(parts, axis=0)
    tiles = []
    lower = (lax.broadcasted_iota(jnp.int32, (8, 1), 0) & distance) == 0
    for i in range(0, rows, 8):
        tile = value[i : i + 8]
        ahead = pltpu.roll(tile, 8 - distance, 0)
        if distance == 4:
            tiles.append(ahead)
        else:
            tiles.append(jnp.where(lower, ahead, pltpu.roll(tile, distance, 0)))
    return jnp.concatenate(tiles, axis=0)


def swap_into(target, value, step, strides):
    for index, stride in enumerate(strides):

        @pl.when(step == index)
        def _():
            target[...] = swap_rows(value, stride)


def tiled_rows(value, count):
    return jnp.concatenate([value] * count, axis=0)


def forward_kernel(strides, groups, each, x_ref, order_ref, after_ref,
                   z_ref, kept_ref, trig_ref, now, swapped, dense, angles):
    step = pl.program_id(0)
    width = order_ref.shape[2]
    rows = groups * each
    parts = width // LANES
    stride = lax.shift_right_logical(jnp.int32(strides[0]), step)

    @pl.when(step == 0)
    def _():
        dense[:, : x_ref.shape[1], :] = x_ref[...].astype(F32)
        for part in range(x_ref.shape[1] // parts):
            for lane in range(parts):
                piece = dense[:, part * parts + lane, :]
                lanes = slice(lane * LANES, (lane + 1) * LANES)
                if part < each:
                    now[part * groups : (part + 1) * groups, lanes] = piece
                else:
                    angles[part - each, :, lanes] = piece

    matrix = one_hot(order_ref[0])
    value = jnp.concatenate([now[...], angles[step]], axis=0)
    upper = upper_rows(rows + groups, groups, stride)
    value = jnp.where(upper, permuted(value, matrix, False), value)
    swap_into(swapped, value, step, strides)
    turned = value[rows:] + swapped[rows:]
    cosine = jnp.cos(turned)
    sine = jnp.sin(turned)
    sine = jnp.where(upper[rows:], sine, -sine)
    trig_ref[0, :groups] = cosine
    trig_ref[0, groups:] = sine
    value = tiled_rows(cosine, each) * value[:rows] + tiled_rows(sine, each) * swapped[:rows]
    kept_ref[0] = value.astype(BF16)
    value = jnp.where(upper[:rows], permuted(value, matrix, True), value)
    now[...] = value

    @pl.when(step == len(strides) - 1)
    def _():
        for part in range(each * parts):
            row, lane = part // parts * groups, part % parts * LANES
            dense[:, part, :] = value[row : row + groups, lane : lane + LANES]
        for side in range(z_ref.shape[0]):
            z_ref[side] = dense[:, : each * parts, :].astype(BF16)


def pack_kernel(in_ref, after_ref, out_ref, dense):
    value = in_ref[...].astype(F32)
    top = jnp.max(jnp.abs(value), axis=(0, 1))
    top = jnp.max(jnp.max(top, axis=0, keepdims=True), axis=1, keepdims=True)
    scale = jnp.ones_like(top)
    exponent = jnp.zeros_like(top)
    for size in STEPS:
        fits = top * scale * 2.0**size < 2.0**15
        scale = jnp.where(fits, scale * 2.0**size, scale)
        exponent = jnp.where(fits, exponent + size, exponent)
    dense[...] = value * scale.reshape(1, 1, 1, 1)
    sides, rows, parts, _ = in_ref.shape
    for part in range(sides * parts):
        out_ref[:, part * LANES : (part + 1) * LANES] = dense[
            part // parts, :, part % parts, :
        ].astype(BF16)
    out_ref[:, sides * parts * LANES :] = jnp.broadcast_to(exponent, (rows, LANES)).astype(BF16)


def pack(array, after):
    sides, rows, parts, _ = array.shape
    return pl.pallas_call(
        pack_kernel,
        in_specs=[
            pl.BlockSpec(memory_space=pltpu.VMEM),
            pl.BlockSpec(memory_space=pl.ANY),
        ],
        out_shape=jax.ShapeDtypeStruct((rows, (sides * parts + 1) * LANES), BF16),
        scratch_shapes=[pltpu.VMEM(array.shape, F32)],
        name="pack",
    )(array, after)


def backward_kernel(strides, groups, each, side_ref, g_ref, own_ref, other_ref, trig_ref, order_ref,
                    sum_ref, now, swapped, dense, sums_out):
    step = pl.program_id(0)
    width = own_ref.shape[2]
    rows = groups * each
    parts = width // LANES
    stride = lax.shift_left(jnp.int32(strides[-1]), step)

    @pl.when(step == 0)
    def _():
        dense[...] = g_ref[...].astype(F32)
        for part in range(each * parts):
            row, lane = part // parts * groups, part % parts * LANES
            now[row : row + groups, lane : lane + LANES] = dense[:, part, :]

    matrix = one_hot(order_ref[0])
    upper = upper_rows(rows + groups, groups, stride)
    value = now[...]
    value = jnp.where(upper[:rows], permuted(value, matrix, False), value)
    own, other = own_ref[0].astype(F32), other_ref[0].astype(F32)
    first = side_ref[0] == 0
    kept = jnp.concatenate([jnp.where(first, own, other), jnp.where(first, other, own)], axis=0)
    swap_into(swapped, jnp.concatenate([value, kept], axis=0), step, strides[::-1])
    partner = swapped[:rows]
    terms = partner * kept - value * swapped[rows:]
    sums = terms[:groups]
    for part in range(1, each):
        sums = sums + terms[part * groups : (part + 1) * groups]
    sums = jnp.where(upper[rows:], -sums, sums)
    cosine, sine = trig_ref[0, :groups], trig_ref[0, groups:]
    before = tiled_rows(cosine, each) * value - tiled_rows(sine, each) * partner
    value = jnp.concatenate([before, sums], axis=0)
    value = jnp.where(upper, permuted(value, matrix, True), value)
    now[...] = value[:rows]
    for index in range(len(strides)):

        @pl.when(step == len(strides) - 1 - index)
        def _():
            for part in range(parts):
                sums_out[:, index * parts + part, :] = value[
                    rows:, part * LANES : (part + 1) * LANES
                ]

    @pl.when(step == len(strides) - 1)
    def _():
        for side in range(sum_ref.shape[0]):
            sum_ref[side] = sums_out[...].astype(BF16)


def turn_forward(strides, groups, each, sides, x, order, after):
    sections, _, width = order.shape
    rows = groups * each
    return pl.pallas_call(
        functools.partial(forward_kernel, strides, groups, each),
        grid=(sections,),
        in_specs=[
            pl.BlockSpec(x.shape, lambda s: (0, 0, 0)),
            pl.BlockSpec((1, 1, width), lambda s: (s, 0, 0)),
            pl.BlockSpec(memory_space=pl.ANY),
        ],
        out_specs=[
            pl.BlockSpec((sides, groups, each * width // LANES, LANES), lambda s: (0, 0, 0, 0)),
            pl.BlockSpec((1, rows, width), lambda s: (s, 0, 0)),
            pl.BlockSpec((1, 2 * groups, width), lambda s: (s, 0, 0)),
        ],
        out_shape=[
            jax.ShapeDtypeStruct((sides, groups, each * width // LANES, LANES), BF16),
            jax.ShapeDtypeStruct((sections, rows, width), BF16),
            jax.ShapeDtypeStruct((sections, 2 * groups, width), F32),
        ],
        scratch_shapes=[
            pltpu.VMEM((rows, width), F32),
            pltpu.VMEM((rows + groups, width), F32),
            pltpu.VMEM((groups, max(x.shape[1], each * width // LANES), LANES), F32),
            pltpu.VMEM((sections, groups, width), F32),
        ],
        compiler_params=pltpu.CompilerParams(vmem_limit_bytes=VMEM),
        cost_estimate=pl.CostEstimate(
            flops=sections * 8 * rows * width * width, bytes_accessed=4 << 20, transcendentals=0
        ),
        name="turn_forward",
    )(x, order, after)


def turn_backward(strides, groups, each, sides, side, g, own, other, trig, order):
    sections, _, width = order.shape
    rows = groups * each
    last = sections - 1
    return pl.pallas_call(
        functools.partial(backward_kernel, strides, groups, each),
        grid=(sections,),
        in_specs=[
            pl.BlockSpec(memory_space=pltpu.SMEM),
            pl.BlockSpec(g.shape, lambda s: (0, 0, 0)),
            pl.BlockSpec((1, rows // sides, width), lambda s: (last - s, 0, 0)),
            pl.BlockSpec((1, rows // sides, width), lambda s: (last - s, 0, 0)),
            pl.BlockSpec((1, 2 * groups, width), lambda s: (last - s, 0, 0)),
            pl.BlockSpec((1, 1, width), lambda s: (last - s, 0, 0)),
        ],
        out_specs=pl.BlockSpec(
            (sides, groups, sections * width // LANES, LANES), lambda s: (0, 0, 0, 0)
        ),
        out_shape=jax.ShapeDtypeStruct(
            (sides, groups, sections * width // LANES, LANES), BF16
        ),
        scratch_shapes=[
            pltpu.VMEM((rows, width), F32),
            pltpu.VMEM((2 * rows, width), F32),
            pltpu.VMEM(g.shape, F32),
            pltpu.VMEM((groups, sections * width // LANES, LANES), F32),
        ],
        compiler_params=pltpu.CompilerParams(vmem_limit_bytes=VMEM),
        cost_estimate=pl.CostEstimate(
            flops=sections * 8 * rows * width * width, bytes_accessed=4 << 20, transcendentals=0
        ),
        name="turn_backward",
    )(side, g, own, other, trig, order)


def gradient_kernel(core_ref, cot_ref, weight_ref, *refs):
    out_ref, dense = refs[-2:]
    near, rows, _ = cot_ref.shape
    hidden, width = weight_ref.shape
    few = out_ref.shape[2]
    parts = width // LANES
    for part in range(rows // few):
        out = product(
            cot_ref[:, part * few : (part + 1) * few, -hidden:].reshape(near * few, hidden),
            weight_ref[...],
            False,
        )
        for lane in range(parts):
            dense[:, part * parts + lane, :] = out[:, lane * LANES : (lane + 1) * LANES]
    out_ref[...] = dense[...].astype(BF16).reshape(out_ref.shape)


def gradient_half(core, cot, weight, each, before=None, after=None):
    near, rows, lanes = cot.shape
    hidden, width = weight.shape
    few = rows // each
    high = each * width // LANES
    in_specs = [
        pl.BlockSpec((near, rows // 2, lanes), lambda e, c: (0, e, 0)),
        pl.BlockSpec((hidden, width), lambda e, c: (0, 0)),
    ]
    operands = [core, cot, weight]
    aliases = {}
    if before is not None:
        in_specs.append(pl.BlockSpec(memory_space=pl.ANY))
        operands.append(before)
        aliases = {3: 0}
    if after is not None:
        in_specs.append(pl.BlockSpec(memory_space=pl.ANY))
        operands.append(after)
    return pl.pallas_call(
        gradient_kernel,
        grid_spec=pltpu.PrefetchScalarGridSpec(
            num_scalar_prefetch=1,
            grid=(2,),
            in_specs=in_specs,
            out_specs=pl.BlockSpec(
                (near, 1, few, high // 2, LANES), lambda e, c: (0, c[0], 0, e, 0)
            ),
            scratch_shapes=[pltpu.VMEM((near * few, high // 2, LANES), F32)],
        ),
        out_shape=jax.ShapeDtypeStruct((near, 2, few, high, LANES), BF16),
        input_output_aliases=aliases,
        compiler_params=pltpu.CompilerParams(vmem_limit_bytes=VMEM),
        cost_estimate=pl.CostEstimate(
            flops=2 * near * rows * hidden * width, bytes_accessed=4 << 20, transcendentals=0
        ),
        name="gradient_half",
    )(*operands)


def projected_kernel(core_ref, token_ref, exponent_ref, weight_ref, *refs):
    out_ref = refs[-1]
    near, _, few, width = token_ref.shape
    tokens = token_ref[...].reshape(near * few, width)
    out = product(tokens, weight_ref[...], True)
    exponent = exponent_ref[...].reshape(near * few, LANES)[:, :1].astype(F32)
    scale = jnp.ones_like(exponent)
    for size in STEPS:
        takes = exponent >= size
        scale = jnp.where(takes, scale * 2.0**-size, scale)
        exponent = jnp.where(takes, exponent - size, exponent)
    out = (out * scale).astype(BF16)
    if len(refs) > 1:
        out = (out.astype(F32) + refs[0][...].reshape(out.shape).astype(F32)).astype(BF16)
    out_ref[...] = out.reshape(out_ref.shape)


def projected_half(core, token_all, weight, each, arrived=None, after=None):
    near, _, few, _ = token_all.shape
    hidden, width = weight.shape
    in_specs = [
        pl.BlockSpec((near, 1, few, width), lambda e, c: (0, c[0], 0, e)),
        pl.BlockSpec((near, 1, few, LANES), lambda e, c: (0, c[0], 0, each * width // LANES)),
        pl.BlockSpec((hidden, width), lambda e, c: (0, 0)),
    ]
    operands = [core, token_all, token_all, weight]
    if arrived is not None:
        in_specs.append(pl.BlockSpec((near, few, hidden), lambda e, c: (0, e, 0)))
        operands.append(arrived)
    if after is not None:
        in_specs.append(pl.BlockSpec(memory_space=pl.ANY))
        operands.append(after)
    return pl.pallas_call(
        projected_kernel,
        grid_spec=pltpu.PrefetchScalarGridSpec(
            num_scalar_prefetch=1,
            grid=(each,),
            in_specs=in_specs,
            out_specs=pl.BlockSpec((near, few, hidden), lambda e, c: (0, e, 0)),
        ),
        out_shape=jax.ShapeDtypeStruct((near, each * few, hidden), BF16),
        compiler_params=pltpu.CompilerParams(vmem_limit_bytes=VMEM),
        cost_estimate=pl.CostEstimate(
            flops=near * few * each * hidden * width // 4, bytes_accessed=1 << 20,
            transcendentals=0,
        ),
        name="projected_half",
    )(*operands)


def sum_kernel(in_ref, out_ref):
    total = jnp.sum(in_ref[...].astype(F32), axis=0).astype(out_ref.dtype)
    for index in range(out_ref.shape[0]):
        out_ref[index] = total


def sum_copies(array, count):
    return pl.pallas_call(
        sum_kernel,
        out_shape=jax.ShapeDtypeStruct((count,) + array.shape[1:], array.dtype),
        name="sum_copies",
    )(array)


def per_device(tokens, up_weight, angles, pair_order, cotangent):
    groups = lax.axis_size(TENSOR)
    near = lax.axis_size(NEAR)
    depth = lax.axis_size(Z)
    sides = lax.axis_size("xh")
    hidden, width = up_weight.shape
    sections = pair_order.shape[0]
    strides = [groups >> (s + 1) for s in range(sections)]
    own_rows = tokens.shape[0] // groups
    each = sides * own_rows
    core = lax.axis_index("c").astype(jnp.int32).reshape(1)
    other_core = [(0, 1), (1, 0)]
    order = pair_order.reshape(sections, 1, width)

    parts = width // LANES
    few = tokens.reshape(own_rows, near, 2, width).transpose(1, 2, 0, 3)
    few = few.reshape(near, 2 * own_rows, width)
    few = jnp.concatenate([few, copies(angles.astype(BF16)[None], near)], axis=1)
    few = few.reshape(near, (2 * own_rows + sections) * parts, LANES)
    mine = jnp.concatenate([few, copies(cotangent[None], near)], axis=2)
    cot_own = all_to_all(mine, NEAR)
    cot_other = lax.ppermute(cot_own, "c", other_core)

    def of_this_core(array):
        start = core[0] * own_rows * parts
        return jnp.concatenate(
            [
                lax.dynamic_slice_in_dim(array[:, :, :LANES], start, own_rows * parts, 1),
                array[:, 2 * own_rows * parts :, :LANES],
            ],
            axis=1,
        )

    def in_order(which, own, other, axis):
        return jnp.stack(
            [jnp.where(which == 0, own, other), jnp.where(which == 0, other, own)], axis=axis
        )

    x = in_order(core[0], of_this_core(cot_own), of_this_core(cot_other), 1)
    x = x.reshape(groups, (own_rows + sections) * parts, LANES)

    part = gradient_half(core, cot_own, up_weight, each)
    part = gradient_half(1 - core, cot_other, up_weight, each, part)
    gradient = lax.psum_scatter(
        part.reshape(depth * groups, each * width // LANES, LANES),
        Z,
        scatter_dimension=0,
        tiled=True,
    )

    rotated, kept, trig = turn_forward(
        strides, groups, own_rows, sides, x, order, part
    )
    other_kept = lax.ppermute(kept, "xh", other_core)
    back = all_to_all(rotated.reshape((sides * groups,) + rotated.shape[2:]), PLANE)
    back = pack(back.reshape(rotated.shape), other_kept).astype(F16)
    token_all = lax.all_gather(back, Z, axis=0, tiled=True).astype(BF16)
    token_all = token_all.reshape(near, 2, groups, each * width + LANES)

    g = all_to_all(gradient, TENSOR)

    side = lax.axis_index("xh").astype(jnp.int32).reshape(1)
    sums = turn_backward(
        strides, groups, each, sides, side, g, kept, other_kept, trig, order
    )

    sent = projected_half(1 - core, token_all, up_weight, each)
    arrived = lax.ppermute(sent, "c", other_core)
    both = projected_half(core, token_all, up_weight, each, arrived)
    projected = lax.psum_scatter(
        both.reshape(near * each * groups, hidden), NEAR, scatter_dimension=0, tiled=True
    )

    sums = all_to_all(sums.reshape((sides * groups,) + sums.shape[2:]), PLANE)
    sums = all_to_all(sum_copies(sums, depth), Z)
    angle_grads = jnp.sum(sums.astype(F32), axis=0).reshape(sections, width)
    return projected, angle_grads


def solution(mesh):
    fine = jax.sharding.Mesh(
        mesh.devices.reshape(16, 2, 2, 4, 2), ("z", "xh", "xl", "y", "c")
    )
    dp, tensor = ("z", "xh"), TENSOR
    placed = (P(dp, tensor), P(dp, tensor), P(None, tensor), P(), P(tensor, dp))
    return jax.shard_map(
        per_device,
        mesh=fine,
        in_specs=placed,
        out_specs=(P(tensor, dp), P(None, tensor)),
        check_vma=False,
    )
```

time: 1170 us -> 204 us (0.17)
  waiting for transfers between devices: 826 us -> 7.3 us
  local copies, waits for them, and re-layouts: 106 us -> 7.37 us
  Pallas kernels: 0 us -> 30.6 us
  other arithmetic: 30.4 us -> 2.21 us
  starting transfers between devices: 37.5 us -> 13.7 us
  blocking collectives: 144 us -> 126 us
    reduce_scatter x2, waiting for transfers between devices: 651 us -> 0.02 us  [the longest x1 0.02 us: per_device(): lax.psum_scatter(part.reshape(depth * groups, each * width // LANES, LANE...]
    all_gather x2 -> x0, waiting for transfers between devices: 158 us -> none  [the longest x1 148 us: per_device(): token_all = lax.all_gather(rotated, 'dp', axis=0, tiled=True)]
    psum x1 -> x0, blocking collectives: 144 us -> none  [per_device(): angle_grads = lax.psum(own_sums, 'dp')]
    gather x38 -> x0, local copies, waits for them, and re-layouts: 98.8 us -> none  [the longest x8 19.7 us: per_device(): jnp.take(new_partner, inverses[factor], axis=-1)]
    all_to_all x0 -> x4, blocking collectives: none -> 69.7 us  [all_to_all(): return lax.all_to_all(array, axes, 0, 0, tiled=True)]
    all_gather x0 -> x1, blocking collectives: none -> 56.2 us  [per_device(): token_all = lax.all_gather(back, Z, axis=0, tiled=True).astype(BF16)]
    pallas_call x0 -> x8, Pallas kernels: none -> 30.6 us  [the longest x2 7.19 us: projected_half(): pl.pallas_call(projected_kernel, grid_spec=pltpu.PrefetchScalarGridSpec(n...]
    ppermute x12 -> x3, starting transfers between devices: 37.4 us -> 8.69 us  [the longest x1 4.73 us: per_device(): other_kept = lax.ppermute(kept, 'xh', other_core)]
  transfers between devices with their start and end apart: 16 -> 6, of which waited for: 9 -> 3; matrix products, arithmetic and copies ran while one was open for 8% -> 2% of each run, Pallas kernels for 0% -> 13%
where the time goes in v2:
time: 204 us; the launch traced here: 201 us
  blocking collectives  126 us (62%)
  Pallas kernels  30.6 us (15%)
  between operations  14.3 us (7%)
  starting transfers between devices  13.7 us (7%)
  local copies, waits for them, and re-layouts  7.37 us (4%)
  waiting for transfers between devices  7.3 us (4%)
  other arithmetic  2.21 us (1%)
    all_to_all x4, blocking collectives, all_to_all(): return lax.all_to_all(array, axes, 0, 0, tiled=True)  69.7 us
    all_gather x1, blocking collectives, per_device(): token_all = lax.all_gather(back, Z, axis=0, tiled=True).astype(BF16)  56.2 us
    pallas_call x2, Pallas kernels, projected_half(): pl.pallas_call(projected_kernel, grid_spec=pltpu.PrefetchScalarGridSpec(n...  7.19 us
    pallas_call x1, Pallas kernels, turn_backward(): pl.pallas_call(functools.partial(backward_kernel, strides, groups, each),...  7.03 us
    pallas_call x1, Pallas kernels, turn_forward(): pl.pallas_call(functools.partial(forward_kernel, strides, groups, each),...  6.75 us
    pallas_call x2, Pallas kernels, gradient_half(): pl.pallas_call(gradient_kernel, grid_spec=pltpu.PrefetchScalarGridSpec(nu...  6.04 us
    all_to_all x1, starting transfers between devices, all_to_all(): return lax.all_to_all(array, axes, 0, 0, tiled=True)  4.9 us
    ppermute x1, starting transfers between devices, per_device(): other_kept = lax.ppermute(kept, 'xh', other_core)  4.73 us
  transfers between devices with their start and end apart: 6, of which 3 were waited for; matrix products, arithmetic and copies ran while one was open for 2% of the time, Pallas kernels for 13%

profile of v2, /device:TPU:24, one launch (start us, length us, event | category | flops | bytes accessed | tf_op | source)
XLA Modules:
  0.0 201.4 jit_solution(8998029940360183800)
XLA Ops:
  7.2 0.0 reduce-scatter.5.cloned.1.call-start
  7.2 0.9 reshape.169
  8.1 0.1 copy.8
  8.2 0.7 convert_element_type.12
  8.9 0.1 pad_maximum_fusion.2
  9.0 0.1 reshape.172
  9.1 1.0 reshape.173
  10.1 0.0 copy-start
  10.1 0.2 pad_maximum_fusion
  10.3 18.8 %all_to_all.25.cot_ref = bf16[8,64,960]{2,1,0:T(8,128)(2,1)S(1)} all-to-all(bf16[8,64,960]{2,1,0:T(8,128)(2,1)S(1)} %pad_maximum_fusion), channel_id=1, replica_groups=mesh['z'=16,'xh'=2,'xl'=2,'y'=4,'c'=2] {'xl','y'}, dimensions={0} | all-to-all | bytes 1966080 | tf_op jit(solution)/shard_map/all_to_all | solution.py:23
  29.1 1.9 collective-permute-start
  31.0 0.0 copy-done
  31.0 2.5 %gradient_half.2.refs_0_ = bf16[8,2,16,32,128]{4,3,2,1,0:T(8,128)(2,1)S(1)} custom-call(s32[1]{0:T(128)} %bitcast.core_ref, bf16[8,64,960]{2,1,0:T(8,128)(2,1)S(1)} %all_to_all.25.cot_ref, bf16[832,1024]{1,0:T(8,128)(2,1)S(1)} %copy-done), custom_call_target="tpu_custom_call" | custom-call | flops 872415232 | bytes 4194304 | tf_op jit(solution)/shard_map/gradient_half/pallas_call | solution.py:319
  33.6 0.2 collective-permute-done.cot_ref
  33.8 3.5 %gradient_half.3.after_ref = bf16[8,2,16,32,128]{4,3,2,1,0:T(8,128)(2,1)S(1)} custom-call(s32[1]{0:T(128)S(6)} %sub.4.core_ref, bf16[8,64,960]{2,1,0:T(8,128)(2,1)} %collective-permute-done.cot_ref, bf16[832,1024]{1,0:T(8,128)(2,1)S(1)} %copy-done, bf16[8,2,16,32,128]{4,3,2,1,0:T(8,128)(2,1)S(1)} %gradient_half.2.refs_0_), custom_call_target="tpu_custom_call", output_to_operand_aliasing={{}: (3, {})} | custom-call | flops 872415232 | bytes 4194304 | tf_op jit(solution)/shard_map/gradient_half/pallas_call | solution.py:319
  37.3 0.0 copy-start.1
  37.3 1.3 copy-done.1
  38.6 0.0 copy-start.5
  38.6 0.0 reduce-scatter.5.cloned.1.call-update
  38.6 0.0 reduce-scatter.3.cloned.1.call-start
  38.7 0.6 copy-done.5
  39.3 0.0 copy-start.2
  39.5 1.0 slice.18
  40.5 0.9 slice_bitcast_fusion
  41.5 0.0 copy-done.2
  41.5 6.8 %turn_forward.1 = (bf16[2,16,16,128]{3,2,1,0:T(8,128)(2,1)S(1)}, bf16[4,32,1024]{2,1,0:T(8,128)(2,1)S(1)}, f32[4,32,1024]{2,1,0:T(8,128)S(1)}) custom-call(bf16[16,48,128]{2,1,0:T(8,128)(2,1)S(1)} %bitcast.24, s32[4,1,1024]{2,1,0:T(1,128)S(1)} %reshape.175.order_ref, bf16[8,2,16,32,128]{4,3,2,1,0:T(8,128)(2,1)S(1)} %copy-done.2), custom_call_target="tpu_custom_call" | custom-call | flops 1073741824 | bytes 4194304 | tf_op jit(solution)/shard_map/turn_forward/pallas_call | solution.py:217
  48.2 4.7 %collective-permute-start.1 = (bf16[4,32,1024]{2,1,0:T(8,128)(2,1)S(1)}, bf16[4,32,1024]{2,1,0:T(8,128)(2,1)S(1)}, u32[]{:S(2)}, u32[]{:S(2)}) collective-permute-start(bf16[4,32,1024]{2,1,0:T(8,128)(2,1)S(1)} %get-tuple-element.6.own_ref), channel_id=1, source_target_pairs={{0,16},{16,0},{1,17},{17,1},{2,18},{18,2},{3,19},{19,3},{4,20},{20... | collective-permute-start | bytes 786440 | tf_op jit(solution)/shard_map/ppermute | solution.py:457
  53.0 11.9 %all_to_all.26 = bf16[32,16,128]{2,1,0:T(8,128)(2,1)} all-to-all(bf16[32,16,128]{2,1,0:T(8,128)(2,1)S(1)} %bitcast.25), channel_id=1, replica_groups=mesh['z'=16,'xh'=2,'xl'=2,'y'=4,'c'=2] {'xh','xl','y','c'}, dimensions={0} | all-to-all | bytes 262144 | tf_op jit(solution)/shard_map/all_to_all | solution.py:23
  64.9 0.0 collective-permute-done.1.after_ref.other_ref
  64.9 0.0 copy-start.3
  64.9 0.7 copy-done.3
  65.6 2.0 pack.1
  67.5 0.9 convert_element_type.13
  68.5 56.2 %all-gather.1 = f16[256,4224]{1,0:T(8,128)(2,1)S(1)} all-gather(f16[16,4224]{1,0:T(8,128)(2,1)S(1)} %convert_element_type.13), channel_id=1, replica_groups=mesh['z'=16,'xh'=2,'xl'=2,'y'=4,'c'=2] {'z'}, dimensions={0}, use_global_device_ids=true | all-gather | bytes 2297856 | tf_op jit(solution)/shard_map/all_gather | solution.py:460
  124.7 0.2 convert_element_type.14
  124.9 3.2 %projected_half.2 = bf16[8,64,832]{2,1,0:T(8,128)(2,1)S(1)} custom-call(s32[1]{0:T(128)S(6)} %sub.4.core_ref, bf16[8,2,16,4224]{3,2,1,0:T(8,128)(2,1)S(1)} %bitcast.18, bf16[8,2,16,4224]{3,2,1,0:T(8,128)(2,1)S(1)} %bitcast.19, bf16[832,1024]{1,0:T(8,128)(2,1)S(1)} %copy-done), custom_call_target="tpu_custom_call" | custom-call | flops 109051904 | bytes 1048576 | tf_op jit(solution)/shard_map/projected_half/pallas_call | solution.py:372
  128.1 0.0 copy-start.4
  128.2 2.1 %collective-permute-start.2 = (bf16[8,64,832]{2,1,0:T(8,128)(2,1)S(1)}, bf16[8,64,832]{2,1,0:T(8,128)(2,1)S(1)}, u32[]{:S(2)}, u32[]{:S(2)}) collective-permute-start(bf16[8,64,832]{2,1,0:T(8,128)(2,1)S(1)} %projected_half.2), channel_id=1, source_target_pairs={{0,1},{1,0},{2,3},{3,2},{4,5},{5,4},{6,7},{7,6},{8,9},{9,8},{10,11... | collective-permute-start | bytes 2555912 | tf_op jit(solution)/shard_map/ppermute | solution.py:471
  130.2 2.4 %collective-permute-done.2.refs_0_ = bf16[8,64,832]{2,1,0:T(8,128)(2,1)S(1)} collective-permute-done((bf16[8,64,832]{2,1,0:T(8,128)(2,1)S(1)}, bf16[8,64,832]{2,1,0:T(8,128)(2,1)S(1)}, u32[]{:S(2)}, u32[]{:S(2)}) %collective-permute-start.2) | collective-permute-done | bytes 852000 | tf_op jit(solution)/shard_map/ppermute | solution.py:471
  132.7 4.0 %projected_half.3 = bf16[8,64,832]{2,1,0:T(8,128)(2,1)} custom-call(s32[1]{0:T(128)} %bitcast.core_ref, bf16[8,2,16,4224]{3,2,1,0:T(8,128)(2,1)S(1)} %bitcast.20, bf16[8,2,16,4224]{3,2,1,0:T(8,128)(2,1)S(1)} %bitcast.21, bf16[832,1024]{1,0:T(8,128)(2,1)S(1)} %copy-done, bf16[8,64,832]{2,1,0:T(8,128)(2,1)S(1)} %collective-permute-done.2.refs_0_), custom_call_target="tpu_custom_call" | custom-call | flops 109051904 | bytes 1048576 | tf_op jit(solution)/shard_map/projected_half/pallas_call | solution.py:372
  136.6 0.0 reduce-scatter.3.cloned.1.call-update
  136.6 0.0 reduce-scatter.5.cloned.1.call-done
  136.7 4.9 %all-to-all-start.2 = ((bf16[16,32,128]{2,1,0:T(8,128)(2,1)}), bf16[16,32,128]{2,1,0:T(8,128)(2,1)S(1)}, u32[]{:S(2)}, u32[]{:S(2)}) async-start(bf16[16,32,128]{2,1,0:T(8,128)(2,1)} %reduce-scatter.5.cloned.1.call-done), calls=%async_computation.4 | async-start | bytes 262144 | tf_op jit(solution)/shard_map/all_to_all | solution.py:23
  141.6 4.6 %all-to-all-done.2.g_ref = bf16[16,32,128]{2,1,0:T(8,128)(2,1)S(1)} async-done(((bf16[16,32,128]{2,1,0:T(8,128)(2,1)}), bf16[16,32,128]{2,1,0:T(8,128)(2,1)S(1)}, u32[]{:S(2)}, u32[]{:S(2)}) %all-to-all-start.2) | async-done | bytes 131104 | tf_op jit(solution)/shard_map/all_to_all | solution.py:23
  146.2 0.0 copy-done.4
  146.2 7.0 %turn_backward.1 = bf16[2,16,32,128]{3,2,1,0:T(8,128)(2,1)S(1)} custom-call(s32[1]{0:T(128)} %bitcast.11.side_ref, bf16[16,32,128]{2,1,0:T(8,128)(2,1)S(1)} %all-to-all-done.2.g_ref, bf16[4,32,1024]{2,1,0:T(8,128)(2,1)S(1)} %get-tuple-element.6.own_ref, bf16[4,32,1024]{2,1,0:T(8,128)(2,1)S(1)} %copy-done.4, f32[4,32,1024]{2,1,0:T(8,128)S(1)} %get-tuple-element.7.trig_ref, ...), custom_call_target="tpu_custom_call" | custom-call | flops 2147483648 | bytes 4194304 | tf_op jit(solution)/shard_map/turn_backward/pallas_call | solution.py:253
  153.2 17.3 %all_to_all.27.in_ref = bf16[32,32,128]{2,1,0:T(8,128)(2,1)} all-to-all(bf16[32,32,128]{2,1,0:T(8,128)(2,1)S(1)} %bitcast.23), channel_id=1, replica_groups=mesh['z'=16,'xh'=2,'xl'=2,'y'=4,'c'=2] {'xh','xl','y','c'}, dimensions={0} | all-to-all | bytes 524288 | tf_op jit(solution)/shard_map/all_to_all | solution.py:23
  170.6 1.6 sum_copies.1
  172.2 21.7 %all_to_all.28 = bf16[16,32,128]{2,1,0:T(8,128)(2,1)S(1)} all-to-all(bf16[16,32,128]{2,1,0:T(8,128)(2,1)} %sum_copies.1), channel_id=1, replica_groups=mesh['z'=16,'xh'=2,'xl'=2,'y'=4,'c'=2] {'z'}, dimensions={0} | all-to-all | bytes 262144 | tf_op jit(solution)/shard_map/all_to_all | solution.py:23
  193.9 0.6 reshape.183
  194.5 0.0 reduce-scatter.3.cloned.1.call-done
  (11 shorter events, 0.3 us)
Async XLA Ops:
  7.2 129.5 %reduce-scatter.5.cloned.1.call-start = ((), (), s32[]{:S(2)}) async-start(), calls=%async_computation.8 | async-start | bytes 2228224 | tf_op jit(solution)/shard_map/reduce_scatter | solution.py:447
  10.1 20.9 %copy-start = (bf16[832,1024]{1,0:T(8,128)(2,1)S(1)}, bf16[832,1024]{1,0:T(8,128)(2,1)}, u32[]{:S(2)}) copy-start(bf16[832,1024]{1,0:T(8,128)(2,1)} %weight_ref.7) | copy-start | bytes 5111812
  29.1 4.7 %collective-permute-start = (bf16[8,64,960]{2,1,0:T(8,128)(2,1)S(1)}, bf16[8,64,960]{2,1,0:T(8,128)(2,1)}, u32[]{:S(2)}, u32[]{:S(2)}) collective-permute-start(bf16[8,64,960]{2,1,0:T(8,128)(2,1)S(1)} %all_to_all.25.cot_ref), channel_id=1, source_target_pairs={{0,1},{1,0},{2,3},{3,2},{4,5},{5,4},{6,7},{7,6},{8,9},{9,8},{10,11... | collective-permute-start | bytes 2949128 | tf_op jit(solution)/shard_map/ppermute | solution.py:425
  37.3 1.3 copy-start.1
  38.6 0.7 copy-start.5
  38.6 155.9 %reduce-scatter.3.cloned.1.call-start = ((), (), s32[]{:S(2)}) async-start(), calls=%async_computation.7 | async-start | bytes 1032192 | tf_op jit(solution)/shard_map/reduce_scatter | solution.py:473
  39.3 2.1 %copy-start.2 = (bf16[8,2,16,32,128]{4,3,2,1,0:T(8,128)(2,1)S(1)}, bf16[8,2,16,32,128]{4,3,2,1,0:T(8,128)(2,1)}, u32[]{:S(2)}) copy-start(bf16[8,2,16,32,128]{4,3,2,1,0:T(8,128)(2,1)} %copy-done.1) | copy-start | bytes 6291460
  48.2 16.6 %collective-permute-start.1 = (bf16[4,32,1024]{2,1,0:T(8,128)(2,1)S(1)}, bf16[4,32,1024]{2,1,0:T(8,128)(2,1)S(1)}, u32[]{:S(2)}, u32[]{:S(2)}) collective-permute-start(bf16[4,32,1024]{2,1,0:T(8,128)(2,1)S(1)} %get-tuple-element.6.own_ref), channel_id=1, source_target_pairs={{0,16},{16,0},{1,17},{17,1},{2,18},{18,2},{3,19},{19,3},{4,20},{20... | collective-permute-start | bytes 786440 | tf_op jit(solution)/shard_map/ppermute | solution.py:457
  64.9 0.7 copy-start.3
  128.1 18.0 %copy-start.4 = (bf16[4,32,1024]{2,1,0:T(8,128)(2,1)S(1)}, bf16[4,32,1024]{2,1,0:T(8,128)(2,1)}, u32[]{:S(2)}) copy-start(bf16[4,32,1024]{2,1,0:T(8,128)(2,1)} %copy-done.3) | copy-start | bytes 786436
  128.2 4.5 %collective-permute-start.2 = (bf16[8,64,832]{2,1,0:T(8,128)(2,1)S(1)}, bf16[8,64,832]{2,1,0:T(8,128)(2,1)S(1)}, u32[]{:S(2)}, u32[]{:S(2)}) collective-permute-start(bf16[8,64,832]{2,1,0:T(8,128)(2,1)S(1)} %projected_half.2), channel_id=1, source_target_pairs={{0,1},{1,0},{2,3},{3,2},{4,5},{5,4},{6,7},{7,6},{8,9},{9,8},{10,11... | collective-permute-start | bytes 2555912 | tf_op jit(solution)/shard_map/ppermute | solution.py:471
  136.7 9.5 %all-to-all-start.2 = ((bf16[16,32,128]{2,1,0:T(8,128)(2,1)}), bf16[16,32,128]{2,1,0:T(8,128)(2,1)S(1)}, u32[]{:S(2)}, u32[]{:S(2)}) async-start(bf16[16,32,128]{2,1,0:T(8,128)(2,1)} %reduce-scatter.5.cloned.1.call-done), calls=%async_computation.4 | async-start | bytes 262144 | tf_op jit(solution)/shard_map/all_to_all | solution.py:23
Sparse Core Ops, SparseCore 0:
  38.8 79.6 reduce-scatter.4
  136.8 41.3 reduce-scatter.2

commit v3 on v2

v3 whole, which is shorter than its diff:
```python
import functools

import jax
import jax.numpy as jnp
from jax import lax
from jax.experimental import pallas as pl
from jax.experimental.pallas import tpu as pltpu
from jax.sharding import PartitionSpec as P

BF16 = jnp.bfloat16
F16 = jnp.float16
F32 = jnp.float32
Z = "z"
TENSOR = ("xl", "y", "c")
NEAR = ("xl", "y")
PLANE = ("xh", "xl", "y", "c")
STEPS = (64, 32, 16, 8, 4, 2)
LANES = 128
VMEM = 24 << 20


def all_to_all(array, axes):
    return lax.all_to_all(array, axes, 0, 0, tiled=True)


def product(left, right, transposed):
    dims = (((1,), (1 if transposed else 0,)), ((), ()))
    return lax.dot_general(left, right, dims, preferred_element_type=F32)


def permuted(value, order):
    rows, width = value.shape
    tiles = width // LANES
    out = []
    for to in range(tiles):
        index = order[:, to * LANES : (to + 1) * LANES]
        lane = jnp.broadcast_to(index & (LANES - 1), (rows, LANES))
        tile = jnp.broadcast_to(index // LANES, (rows, LANES))
        chosen = None
        for source in range(tiles):
            piece = jnp.take_along_axis(
                value[:, source * LANES : (source + 1) * LANES],
                lane,
                axis=1,
                mode="promise_in_bounds",
            )
            chosen = piece if chosen is None else jnp.where(tile == source, piece, chosen)
        out.append(chosen)
    return jnp.concatenate(out, axis=1)


def inverse_kernel(column_ref, row_ref, out_ref):
    width, sections = column_ref.shape
    row = lax.broadcasted_iota(jnp.int32, (width, width), 0)
    lane = lax.broadcasted_iota(jnp.int32, (width, width), 1)
    for s in range(sections):
        hits = jnp.where(column_ref[:, s : s + 1] == lane, row, 0)
        out_ref[s, 0:1] = row_ref[s : s + 1]
        out_ref[s, 1:2] = jnp.sum(hits, axis=0, keepdims=True)


def with_inverses(order):
    sections, width = order.shape
    return pl.pallas_call(
        inverse_kernel,
        out_shape=jax.ShapeDtypeStruct((sections, 2, width), jnp.int32),
        compiler_params=pltpu.CompilerParams(vmem_limit_bytes=VMEM),
        name="with_inverses",
    )(order.T, order)


def prepare_kernel(token_ref, angle_ref, cot_ref, out_ref, tokens, dense):
    near = out_ref.shape[0]
    groups, width = 2 * near, token_ref.shape[1]
    own_rows = token_ref.shape[0] // groups
    parts = width // LANES
    for part in range(parts):
        lanes = slice(part * LANES, (part + 1) * LANES)
        tokens[part] = token_ref[:, lanes].astype(F32)
        for core in range(2):
            for row in range(own_rows):
                dense[:, (core * own_rows + row) * parts + part, :] = tokens[
                    part, pl.ds(row * groups + core, near, stride=2), :
                ]
        for s in range(angle_ref.shape[0]):
            dense[:, (2 * own_rows + s) * parts + part, :] = jnp.broadcast_to(
                angle_ref[s : s + 1, lanes], (near, LANES)
            )
    out_ref[:, :, :LANES] = dense[...].astype(BF16)
    for index in range(near):
        out_ref[index, :, LANES:] = cot_ref[...]


def prepare(tokens, angles, cotangent, near):
    rows, hidden = cotangent.shape
    return pl.pallas_call(
        prepare_kernel,
        out_shape=jax.ShapeDtypeStruct((near, rows, LANES + hidden), BF16),
        scratch_shapes=[pltpu.VMEM((tokens.shape[1] // LANES, tokens.shape[0], LANES), F32), pltpu.VMEM((near, rows, LANES), F32)],
        compiler_params=pltpu.CompilerParams(vmem_limit_bytes=60 << 20),
        name="prepare",
    )(tokens, angles, cotangent)


def upper_rows(rows, groups, stride):
    group = lax.broadcasted_iota(jnp.int32, (rows, 1), 0) & (groups - 1)
    return (group & stride) != 0


def swap_rows(value, distance):
    rows = value.shape[0]
    if distance >= 8:
        parts = []
        for i in range(0, rows, 2 * distance):
            parts += [value[i + distance : i + 2 * distance], value[i : i + distance]]
        return jnp.concatenate(parts, axis=0)
    tiles = []
    lower = (lax.broadcasted_iota(jnp.int32, (8, 1), 0) & distance) == 0
    for i in range(0, rows, 8):
        tile = value[i : i + 8]
        ahead = pltpu.roll(tile, 8 - distance, 0)
        if distance == 4:
            tiles.append(ahead)
        else:
            tiles.append(jnp.where(lower, ahead, pltpu.roll(tile, distance, 0)))
    return jnp.concatenate(tiles, axis=0)


def swap_into(target, value, step, strides):
    for index, stride in enumerate(strides):

        @pl.when(step == index)
        def _():
            target[...] = swap_rows(value, stride)


def tiled_rows(value, count):
    return jnp.concatenate([value] * count, axis=0)


def forward_kernel(strides, groups, each, core_ref, own_ref, other_ref, order_ref, after_ref,
                   z_ref, kept_ref, trig_ref, now, swapped, dense, angles):
    step = pl.program_id(0)
    width = order_ref.shape[2]
    rows = groups * each
    parts = width // LANES
    stride = lax.shift_right_logical(jnp.int32(strides[0]), step)

    @pl.when(step == 0)
    def _():
        core = core_ref[0]
        tall = each * parts
        for which, ref in ((core, own_ref), (1 - core, other_ref)):
            tokens = ref[:, pl.ds(pl.multiple_of(core * tall, tall), tall), :].astype(F32)
            rest = ref[:, 2 * tall :, :].astype(F32)
            for near in range(groups // 2):
                dense[pl.ds(2 * near + which, 1), :tall] = tokens[near : near + 1]
                dense[pl.ds(2 * near + which, 1), tall:] = rest[near : near + 1]
        for part in range(each + len(strides)):
            for lane in range(parts):
                piece = dense[:, part * parts + lane, :]
                lanes = slice(lane * LANES, (lane + 1) * LANES)
                if part < each:
                    now[part * groups : (part + 1) * groups, lanes] = piece
                else:
                    angles[part - each, :, lanes] = piece

    order, inverse = order_ref[0, 0:1], order_ref[0, 1:2]
    value = jnp.concatenate([now[...], angles[step]], axis=0)
    upper = upper_rows(rows + groups, groups, stride)
    value = jnp.where(upper, permuted(value, order), value)
    swap_into(swapped, value, step, strides)
    turned = value[rows:] + swapped[rows:]
    cosine = jnp.cos(turned)
    sine = jnp.sin(turned)
    sine = jnp.where(upper[rows:], sine, -sine)
    trig_ref[0, :groups] = cosine
    trig_ref[0, groups:] = sine
    value = tiled_rows(cosine, each) * value[:rows] + tiled_rows(sine, each) * swapped[:rows]
    kept_ref[0] = value.astype(BF16)
    value = jnp.where(upper[:rows], permuted(value, inverse), value)
    now[...] = value

    @pl.when(step == len(strides) - 1)
    def _():
        for part in range(each * parts):
            row, lane = part // parts * groups, part % parts * LANES
            dense[:, part, :] = value[row : row + groups, lane : lane + LANES]
        for side in range(z_ref.shape[0]):
            z_ref[side] = dense[:, : each * parts, :].astype(BF16)


def pack_kernel(in_ref, out_ref, dense):
    value = in_ref[...].astype(F32)
    top = jnp.max(jnp.abs(value), axis=(0, 1))
    top = jnp.max(jnp.max(top, axis=0, keepdims=True), axis=1, keepdims=True)
    scale = jnp.ones_like(top)
    exponent = jnp.zeros_like(top)
    for size in STEPS:
        fits = top * scale * 2.0**size < 2.0**15
        scale = jnp.where(fits, scale * 2.0**size, scale)
        exponent = jnp.where(fits, exponent + size, exponent)
    dense[...] = value * scale.reshape(1, 1, 1, 1)
    sides, rows, parts, _ = in_ref.shape
    for part in range(sides * parts):
        out_ref[:, part * LANES : (part + 1) * LANES] = dense[
            part // parts, :, part % parts, :
        ].astype(BF16)
    out_ref[:, sides * parts * LANES :] = jnp.broadcast_to(exponent, (rows, LANES)).astype(BF16)


def pack(array):
    sides, rows, parts, _ = array.shape
    return pl.pallas_call(
        pack_kernel,
        out_shape=jax.ShapeDtypeStruct((rows, (sides * parts + 1) * LANES), BF16),
        scratch_shapes=[pltpu.VMEM(array.shape, F32)],
        name="pack",
    )(array)


def backward_kernel(strides, groups, each, g_ref, kept_ref, trig_ref, order_ref,
                    sum_ref, now, swapped, dense, sums_out):
    step = pl.program_id(0)
    width = kept_ref.shape[2]
    rows = groups * each
    parts = width // LANES
    stride = lax.shift_left(jnp.int32(strides[-1]), step)

    @pl.when(step == 0)
    def _():
        dense[...] = jnp.sum(g_ref[...].astype(F32), axis=0)
        for part in range(each * parts):
            row, lane = part // parts * groups, part % parts * LANES
            now[row : row + groups, lane : lane + LANES] = dense[:, part, :]

    order, inverse = order_ref[0, 0:1], order_ref[0, 1:2]
    upper = upper_rows(rows + groups, groups, stride)
    value = now[...]
    value = jnp.where(upper[:rows], permuted(value, order), value)
    kept = kept_ref[0].astype(F32)
    swap_into(swapped, jnp.concatenate([value, kept], axis=0), step, strides[::-1])
    partner = swapped[:rows]
    terms = partner * kept - value * swapped[rows:]
    sums = terms[:groups]
    for part in range(1, each):
        sums = sums + terms[part * groups : (part + 1) * groups]
    sums = jnp.where(upper[rows:], -sums, sums)
    cosine, sine = trig_ref[0, :groups], trig_ref[0, groups:]
    before = tiled_rows(cosine, each) * value - tiled_rows(sine, each) * partner
    value = jnp.concatenate([before, sums], axis=0)
    value = jnp.where(upper, permuted(value, inverse), value)
    now[...] = value[:rows]
    for index in range(len(strides)):

        @pl.when(step == len(strides) - 1 - index)
        def _():
            for part in range(parts):
                sums_out[:, index * parts + part, :] = value[
                    rows:, part * LANES : (part + 1) * LANES
                ]

    @pl.when(step == len(strides) - 1)
    def _():
        for side in range(sum_ref.shape[0]):
            sum_ref[side] = sums_out[...].astype(BF16)


def turn_forward(strides, groups, each, sides, core, own, other, order, after):
    sections, _, width = order.shape
    rows = groups * each
    near, high, _ = own.shape
    return pl.pallas_call(
        functools.partial(forward_kernel, strides, groups, each),
        grid=(sections,),
        in_specs=[
            pl.BlockSpec(memory_space=pltpu.SMEM),
            pl.BlockSpec((near, high, LANES), lambda s: (0, 0, 0)),
            pl.BlockSpec((near, high, LANES), lambda s: (0, 0, 0)),
            pl.BlockSpec((1, 2, width), lambda s: (s, 0, 0)),
            pl.BlockSpec(memory_space=pl.ANY),
        ],
        out_specs=[
            pl.BlockSpec((sides, groups, each * width // LANES, LANES), lambda s: (0, 0, 0, 0)),
            pl.BlockSpec((1, rows, width), lambda s: (s, 0, 0)),
            pl.BlockSpec((1, 2 * groups, width), lambda s: (s, 0, 0)),
        ],
        out_shape=[
            jax.ShapeDtypeStruct((sides, groups, each * width // LANES, LANES), BF16),
            jax.ShapeDtypeStruct((sections, rows, width), BF16),
            jax.ShapeDtypeStruct((sections, 2 * groups, width), F32),
        ],
        scratch_shapes=[
            pltpu.VMEM((rows, width), F32),
            pltpu.VMEM((rows + groups, width), F32),
            pltpu.VMEM((groups, (each + sections) * width // LANES, LANES), F32),
            pltpu.VMEM((sections, groups, width), F32),
        ],
        compiler_params=pltpu.CompilerParams(vmem_limit_bytes=VMEM),
        cost_estimate=pl.CostEstimate(
            flops=sections * 8 * rows * width * width, bytes_accessed=4 << 20, transcendentals=0
        ),
        name="turn_forward",
    )(core, own, other, order, after)


def turn_backward(strides, groups, each, sides, g, kept, trig, order):
    sections, _, width = order.shape
    rows = groups * each
    last = sections - 1
    return pl.pallas_call(
        functools.partial(backward_kernel, strides, groups, each),
        grid=(sections,),
        in_specs=[
            pl.BlockSpec(g.shape, lambda s: (0, 0, 0, 0)),
            pl.BlockSpec((1, rows, width), lambda s: (last - s, 0, 0)),
            pl.BlockSpec((1, 2 * groups, width), lambda s: (last - s, 0, 0)),
            pl.BlockSpec((1, 2, width), lambda s: (last - s, 0, 0)),
        ],
        out_specs=pl.BlockSpec(
            (sides, groups, sections * width // LANES, LANES), lambda s: (0, 0, 0, 0)
        ),
        out_shape=jax.ShapeDtypeStruct(
            (sides, groups, sections * width // LANES, LANES), BF16
        ),
        scratch_shapes=[
            pltpu.VMEM((rows, width), F32),
            pltpu.VMEM((2 * rows, width), F32),
            pltpu.VMEM(g.shape[1:], F32),
            pltpu.VMEM((groups, sections * width // LANES, LANES), F32),
        ],
        compiler_params=pltpu.CompilerParams(vmem_limit_bytes=VMEM),
        cost_estimate=pl.CostEstimate(
            flops=sections * 8 * rows * width * width, bytes_accessed=4 << 20, transcendentals=0
        ),
        name="turn_backward",
    )(g, kept, trig, order)


def gradient_kernel(core_ref, own_ref, other_ref, weight_ref, after_ref, out_ref):
    near, rows, _ = own_ref.shape
    hidden, width = weight_ref.shape
    core = core_ref[0]
    for which, ref in ((core, own_ref), (1 - core, other_ref)):
        out = product(
            ref[:, :, -hidden:].reshape(near * rows, hidden), weight_ref[...], False
        )
        out_ref[:, pl.ds(which, 1)] = out.astype(BF16).reshape(near, 1, rows, width)


def gradient(core, own, other, weight, after):
    near, rows, lanes = own.shape
    hidden, width = weight.shape
    steps = 2
    return pl.pallas_call(
        gradient_kernel,
        grid=(steps,),
        in_specs=[
            pl.BlockSpec(memory_space=pltpu.SMEM),
            pl.BlockSpec((near, rows // steps, lanes), lambda e: (0, e, 0)),
            pl.BlockSpec((near, rows // steps, lanes), lambda e: (0, e, 0)),
            pl.BlockSpec((hidden, width), lambda e: (0, 0)),
            pl.BlockSpec(memory_space=pl.ANY),
        ],
        out_specs=pl.BlockSpec((near, 2, rows // steps, width), lambda e: (0, 0, e, 0)),
        out_shape=jax.ShapeDtypeStruct((near, 2, rows, width), BF16),
        compiler_params=pltpu.CompilerParams(vmem_limit_bytes=VMEM),
        cost_estimate=pl.CostEstimate(
            flops=4 * near * rows * hidden * width, bytes_accessed=6 << 20, transcendentals=0
        ),
        name="gradient",
    )(core, own, other, weight, after)


def spread_kernel(in_ref, out_ref, dense):
    groups = out_ref.shape[1]
    parts = in_ref.shape[1] // LANES
    own_rows = out_ref.shape[2] // parts
    for side in range(out_ref.shape[0]):
        for row in range(own_rows):
            first = (side * own_rows + row) * groups
            for part in range(parts):
                dense[side, :, row * parts + part, :] = in_ref[
                    first : first + groups, part * LANES : (part + 1) * LANES
                ].astype(F32)
    out_ref[...] = dense[...].astype(BF16)


def spread(array, sides, groups):
    rows, width = array.shape
    shape = (sides, groups, rows // (sides * groups) * width // LANES, LANES)
    return pl.pallas_call(
        spread_kernel,
        out_shape=jax.ShapeDtypeStruct(shape, BF16),
        scratch_shapes=[pltpu.VMEM(shape, F32)],
        name="spread",
    )(array)


def projected_kernel(core_ref, token_ref, exponent_ref, weight_ref, *refs):
    out_ref = refs[-1]
    near, _, few, lanes = token_ref.shape
    width = weight_ref.shape[1]
    parts = lanes // width
    tokens = jnp.concatenate(
        [
            token_ref[:, :, :, part * width : (part + 1) * width].reshape(near * few, width)
            for part in range(parts)
        ],
        axis=0,
    )
    out = product(tokens, weight_ref[...], True)
    exponent = exponent_ref[...].reshape(near * few, LANES)[:, :1].astype(F32)
    scale = jnp.ones_like(exponent)
    for size in STEPS:
        takes = exponent >= size
        scale = jnp.where(takes, scale * 2.0**-size, scale)
        exponent = jnp.where(takes, exponent - size, exponent)
    for part in range(parts):
        piece = (out[part * near * few : (part + 1) * near * few] * scale).astype(BF16)
        piece = piece.reshape(near, few, piece.shape[1])
        rows = slice(part * few, (part + 1) * few)
        if len(refs) > 1:
            piece = (piece.astype(F32) + refs[0][:, rows].astype(F32)).astype(BF16)
        out_ref[:, rows] = piece


def projected_half(core, token_all, weight, each, arrived=None, after=None):
    near, _, few, _ = token_all.shape
    hidden, width = weight.shape
    steps = 2
    at_once = each // steps
    in_specs = [
        pl.BlockSpec((near, 1, few, at_once * width), lambda e, c: (0, c[0], 0, e)),
        pl.BlockSpec((near, 1, few, LANES), lambda e, c: (0, c[0], 0, each * width // LANES)),
        pl.BlockSpec((hidden, width), lambda e, c: (0, 0)),
    ]
    operands = [core, token_all, token_all, weight]
    if arrived is not None:
        in_specs.append(pl.BlockSpec((near, at_once * few, hidden), lambda e, c: (0, e, 0)))
        operands.append(arrived)
        in_specs.append(pl.BlockSpec(memory_space=pl.ANY))
        operands.append(after)
    return pl.pallas_call(
        projected_kernel,
        grid_spec=pltpu.PrefetchScalarGridSpec(
            num_scalar_prefetch=1,
            grid=(steps,),
            in_specs=in_specs,
            out_specs=pl.BlockSpec((near, at_once * few, hidden), lambda e, c: (0, e, 0)),
        ),
        out_shape=jax.ShapeDtypeStruct((near, each * few, hidden), BF16),
        compiler_params=pltpu.CompilerParams(vmem_limit_bytes=VMEM),
        cost_estimate=pl.CostEstimate(
            flops=near * few * each * hidden * width // 4, bytes_accessed=1 << 20,
            transcendentals=0,
        ),
        name="projected_half",
    )(*operands)


def sum_kernel(in_ref, out_ref):
    total = jnp.sum(in_ref[...].astype(F32), axis=0).astype(out_ref.dtype)
    for index in range(out_ref.shape[0]):
        out_ref[index] = total


def sum_copies(array, count):
    return pl.pallas_call(
        sum_kernel,
        out_shape=jax.ShapeDtypeStruct((count,) + array.shape[1:], array.dtype),
        name="sum_copies",
    )(array)


def per_device(tokens, up_weight, angles, pair_order, cotangent):
    groups = lax.axis_size(TENSOR)
    near = lax.axis_size(NEAR)
    depth = lax.axis_size(Z)
    sides = lax.axis_size("xh")
    hidden, width = up_weight.shape
    sections = pair_order.shape[0]
    strides = [groups >> (s + 1) for s in range(sections)]
    own_rows = tokens.shape[0] // groups
    each = sides * own_rows
    core = lax.axis_index("c").astype(jnp.int32).reshape(1)
    other_core = [(0, 1), (1, 0)]
    order = with_inverses(pair_order)

    mine = prepare(tokens, angles, cotangent, near)
    cot_own = all_to_all(mine, NEAR)
    cot_other = lax.ppermute(cot_own, "c", other_core)

    part = gradient(core, cot_own, cot_other, up_weight, order)
    summed = lax.psum_scatter(
        part.reshape(depth * part.shape[2], width), Z, scatter_dimension=0, tiled=True
    )

    rotated, kept, trig = turn_forward(
        strides, groups, own_rows, sides, core, cot_own, cot_other, order, part
    )
    back = all_to_all(rotated.reshape((sides * groups,) + rotated.shape[2:]), PLANE)
    back = pack(back.reshape(rotated.shape)).astype(F16)
    token_all = lax.all_gather(back, Z, axis=0, tiled=True).astype(BF16)
    token_all = token_all.reshape(near, 2, groups, each * width + LANES)

    g = spread(summed, sides, groups)

    sent = projected_half(1 - core, token_all, up_weight, each)
    arrived = lax.ppermute(sent, "c", other_core)
    both = projected_half(core, token_all, up_weight, each, arrived, g)
    projected = lax.psum_scatter(
        both.reshape(near * each * groups, hidden), NEAR, scatter_dimension=0, tiled=True
    )

    g = all_to_all(g.reshape((sides * groups,) + g.shape[2:]), PLANE).reshape(rotated.shape)
    sums = turn_backward(strides, groups, own_rows, sides, g, kept, trig, order)

    sums = all_to_all(sums.reshape((sides * groups,) + sums.shape[2:]), PLANE)
    sums = all_to_all(sum_copies(sums, depth), Z)
    angle_grads = jnp.sum(sums.astype(F32), axis=0).reshape(sections, width)
    return projected, angle_grads


def solution(mesh):
    fine = jax.sharding.Mesh(
        mesh.devices.reshape(16, 2, 2, 4, 2), ("z", "xh", "xl", "y", "c")
    )
    dp, tensor = ("z", "xh"), TENSOR
    placed = (P(dp, tensor), P(dp, tensor), P(None, tensor), P(), P(tensor, dp))
    return jax.shard_map(
        per_device,
        mesh=fine,
        in_specs=placed,
        out_specs=(P(tensor, dp), P(None, tensor)),
        check_vma=False,
    )
```

time: 204 us -> 200 us (0.980)
  starting transfers between devices: 13.7 us -> 11 us
    ppermute x1 -> x0, starting transfers between devices: 4.73 us -> none  [per_device(): other_kept = lax.ppermute(kept, 'xh', other_core)]
    pallas_call x3 -> x5, Pallas kernels: 8 us -> 12.7 us  [the longest x1 4.58 us: gradient(): pl.pallas_call(gradient_kernel, grid=(steps,), in_specs=[pl.BlockSpec(mem...]
    unnamed x12 -> x23, local copies, waits for them, and re-layouts: 2.68 us -> 7.15 us
    pallas_call x1, Pallas kernels: 7.03 us -> 3.94 us  [turn_backward(): pl.pallas_call(functools.partial(backward_kernel, strides, groups, each),...]
    all_to_all x1, starting transfers between devices: 4.9 us -> 7.07 us  [all_to_all(): return lax.all_to_all(array, axes, 0, 0, tiled=True)]
    pallas_call x2, Pallas kernels: 7.19 us -> 5.07 us  [projected_half(): pl.pallas_call(projected_kernel, grid_spec=pltpu.PrefetchScalarGridSpec(n...]
  transfers between devices with their start and end apart: 6 -> 5, of which waited for: 3 -> 3; matrix products, arithmetic and copies ran while one was open for 2% -> 1% of each run, Pallas kernels for 13% -> 10%
where the time goes in v3:
time: 200 us; the launch traced here: 199 us
  blocking collectives  128 us (64%)
  Pallas kernels  29.8 us (15%)
  between operations  14.2 us (7%)
  starting transfers between devices  11 us (6%)
  local copies, waits for them, and re-layouts  7.76 us (4%)
  waiting for transfers between devices  7.37 us (4%)
    all_to_all x4, blocking collectives, all_to_all(): return lax.all_to_all(array, axes, 0, 0, tiled=True)  69.7 us
    all_gather x1, blocking collectives, per_device(): token_all = lax.all_gather(back, Z, axis=0, tiled=True).astype(BF16)  58 us
    unnamed x23, local copies, waits for them, and re-layouts  7.15 us
    all_to_all x1, starting transfers between devices, all_to_all(): return lax.all_to_all(array, axes, 0, 0, tiled=True)  7.07 us
    pallas_call x1, Pallas kernels, turn_forward(): pl.pallas_call(functools.partial(forward_kernel, strides, groups, each),...  6.42 us
    all_to_all x1, waiting for transfers between devices, all_to_all(): return lax.all_to_all(array, axes, 0, 0, tiled=True)  6.01 us
    pallas_call x2, Pallas kernels, projected_half(): pl.pallas_call(projected_kernel, grid_spec=pltpu.PrefetchScalarGridSpec(n...  5.07 us
    pallas_call x1, Pallas kernels, gradient(): pl.pallas_call(gradient_kernel, grid=(steps,), in_specs=[pl.BlockSpec(mem...  4.58 us
  transfers between devices with their start and end apart: 5, of which 3 were waited for; matrix products, arithmetic and copies ran while one was open for 1% of the time, Pallas kernels for 10%

profile of v3, /device:TPU:24, one launch (start us, length us, event | category | flops | bytes accessed | tf_op | source)
XLA Modules:
  0.0 198.9 jit_solution(11682260674993985874)
XLA Ops:
  7.2 0.0 copy-start.5
  7.2 0.0 copy-start
  7.2 0.0 reduce-scatter.3.cloned.1.call-start
  7.2 2.3 %prepare.1 = bf16[8,64,960]{2,1,0:T(8,128)(2,1)} custom-call(bf16[32,1024]{1,0:T(8,128)(2,1)} %token_ref.1, f32[4,1024]{1,0:T(4,128)} %angle_ref.1, bf16[64,832]{1,0:T(8,128)(2,1)} %cot_ref.1), custom_call_target="tpu_custom_call" | custom-call | tf_op jit(solution)/shard_map/prepare/pallas_call | solution.py:96
  9.6 18.8 %all_to_all.25.own_ref = bf16[8,64,960]{2,1,0:T(8,128)(2,1)S(1)} all-to-all(bf16[8,64,960]{2,1,0:T(8,128)(2,1)} %prepare.1), channel_id=1, replica_groups=mesh['z'=16,'xh'=2,'xl'=2,'y'=4,'c'=2] {'xl','y'}, dimensions={0} | all-to-all | bytes 1966080 | tf_op jit(solution)/shard_map/all_to_all | solution.py:23
  28.4 1.9 collective-permute-start
  30.3 0.0 copy-done.5
  30.3 0.2 copy.7
  30.6 2.1 %with_inverses.1.after_ref.order_ref = s32[4,2,1024]{2,1,0:T(2,128)S(1)} custom-call(s32[1024,4]{1,0:T(8,128)S(1)} %bitcast.14, s32[4,1024]{1,0:T(4,128)S(1)} %copy-done.5), custom_call_target="tpu_custom_call" | custom-call | tf_op jit(solution)/shard_map/with_inverses/pallas_call | solution.py:64
  32.7 0.4 collective-permute-done.other_ref
  33.1 0.0 copy-done
  33.1 4.6 %gradient.1.after_ref = bf16[8,2,64,1024]{3,2,1,0:T(8,128)(2,1)} custom-call(s32[1]{0:T(128)} %bitcast.core_ref, bf16[8,64,960]{2,1,0:T(8,128)(2,1)S(1)} %all_to_all.25.own_ref, bf16[8,64,960]{2,1,0:T(8,128)(2,1)} %collective-permute-done.other_ref, bf16[832,1024]{1,0:T(8,128)(2,1)S(1)} %copy-done, s32[4,2,1024]{2,1,0:T(2,128)S(1)} %with_inverses.1.after_ref.order_ref), custom_call_target="tpu_custom_call" | custom-call | flops 1744830464 | bytes 6291456 | tf_op jit(solution)/shard_map/gradient/pallas_call | solution.py:355
  37.7 0.0 reduce-scatter.3.cloned.1.call-update
  37.7 6.4 %turn_forward.1 = (bf16[2,16,16,128]{3,2,1,0:T(8,128)(2,1)}, bf16[4,32,1024]{2,1,0:T(8,128)(2,1)S(1)}, f32[4,32,1024]{2,1,0:T(8,128)S(1)}) custom-call(s32[1]{0:T(128)} %bitcast.core_ref, bf16[8,64,960]{2,1,0:T(8,128)(2,1)S(1)} %all_to_all.25.own_ref, bf16[8,64,960]{2,1,0:T(8,128)(2,1)} %collective-permute-done.other_ref, ...), custom_call_target="tpu_custom_call" | custom-call | flops 1073741824 | bytes 4194304 | tf_op jit(solution)/shard_map/turn_forward/pallas_call | solution.py:273
  44.1 0.0 copy-start.8
  44.1 0.7 copy-done.8
  44.8 0.0 copy-start.6
  44.8 7.1 %all-to-all-start.1 = ((bf16[32,16,128]{2,1,0:T(8,128)(2,1)}), bf16[32,16,128]{2,1,0:T(8,128)(2,1)S(1)}, u32[]{:S(2)}, u32[]{:S(2)}) async-start(bf16[32,16,128]{2,1,0:T(8,128)(2,1)} %bitcast.2), calls=%async_computation.1 | async-start | bytes 262144 | tf_op jit(solution)/shard_map/all_to_all | solution.py:23
  51.9 0.0 reduce-scatter.5.cloned.1.call-start
  51.9 6.0 %all-to-all-done.1 = bf16[32,16,128]{2,1,0:T(8,128)(2,1)S(1)} async-done(((bf16[32,16,128]{2,1,0:T(8,128)(2,1)}), bf16[32,16,128]{2,1,0:T(8,128)(2,1)S(1)}, u32[]{:S(2)}, u32[]{:S(2)}) %all-to-all-start.1) | async-done | bytes 131104 | tf_op jit(solution)/shard_map/all_to_all | solution.py:23
  57.9 0.0 copy-start.10
  57.9 0.7 copy-done.10
  58.6 1.9 pack.1
  60.5 0.9 convert_element_type.9
  61.5 58.0 %all-gather.1 = f16[256,4224]{1,0:T(8,128)(2,1)S(1)} all-gather(f16[16,4224]{1,0:T(8,128)(2,1)S(1)} %convert_element_type.9), channel_id=1, replica_groups=mesh['z'=16,'xh'=2,'xl'=2,'y'=4,'c'=2] {'z'}, dimensions={0}, use_global_device_ids=true | all-gather | bytes 2297856 | tf_op jit(solution)/shard_map/all_gather | solution.py:504
  119.4 0.0 copy-start.1
  119.4 0.2 convert_element_type.10
  119.7 0.0 copy-done.6
  119.7 1.2 copy-done.1
  120.9 2.5 %projected_half.2 = bf16[8,64,832]{2,1,0:T(8,128)(2,1)} custom-call(s32[1]{0:T(128)S(6)} %sub.3.core_ref, bf16[8,2,16,4224]{3,2,1,0:T(8,128)(2,1)S(1)} %bitcast.10, bf16[8,2,16,4224]{3,2,1,0:T(8,128)(2,1)S(1)} %bitcast.11, bf16[832,1024]{1,0:T(8,128)(2,1)S(1)} %copy-done.1), custom_call_target="tpu_custom_call" | custom-call | flops 109051904 | bytes 1048576 | tf_op jit(solution)/shard_map/projected_half/pallas_call | solution.py:444
  123.4 1.9 collective-permute-start.1
  125.3 0.0 reduce-scatter.3.cloned.1.call-done.in_ref
  125.3 1.7 spread.1.refs_1_
  127.0 0.9 collective-permute-done.1.refs_0_
  127.9 0.0 copy-start.2
  127.9 1.5 copy-done.2
  129.4 0.0 copy-start.3
  129.4 0.9 copy-done.3
  130.3 0.0 copy-start.4
  130.3 2.6 %projected_half.3 = bf16[8,64,832]{2,1,0:T(8,128)(2,1)} custom-call(s32[1]{0:T(128)} %bitcast.core_ref, bf16[8,2,16,4224]{3,2,1,0:T(8,128)(2,1)S(1)} %bitcast.12, bf16[8,2,16,4224]{3,2,1,0:T(8,128)(2,1)S(1)} %bitcast.13, bf16[832,1024]{1,0:T(8,128)(2,1)S(1)} %copy-done.2, bf16[8,64,832]{2,1,0:T(8,128)(2,1)S(1)} %collective-permute-done.1.refs_0_, ...), custom_call_target="tpu_custom_call" | custom-call | flops 109051904 | bytes 1048576 | tf_op jit(solution)/shard_map/projected_half/pallas_call | solution.py:444
  132.9 0.0 reduce-scatter.5.cloned.1.call-update
  132.9 0.0 copy-done.4
  132.9 13.9 %all_to_all.26 = bf16[32,16,128]{2,1,0:T(8,128)(2,1)S(1)} all-to-all(bf16[32,16,128]{2,1,0:T(8,128)(2,1)S(1)} %bitcast.15), channel_id=1, replica_groups=mesh['z'=16,'xh'=2,'xl'=2,'y'=4,'c'=2] {'xh','xl','y','c'}, dimensions={0} | all-to-all | bytes 262144 | tf_op jit(solution)/shard_map/all_to_all | solution.py:23
  146.8 0.0 copy-start.7
  146.8 1.1 copy-done.7
  147.8 0.0 copy-start.9
  147.9 0.9 copy-done.9
  148.8 3.9 %turn_backward.1 = bf16[2,16,32,128]{3,2,1,0:T(8,128)(2,1)S(1)} custom-call(bf16[2,16,16,128]{3,2,1,0:T(8,128)(2,1)S(1)} %bitcast.17, bf16[4,32,1024]{2,1,0:T(8,128)(2,1)S(1)} %copy-done.9, f32[4,32,1024]{2,1,0:T(8,128)S(1)} %copy-done.7, s32[4,2,1024]{2,1,0:T(2,128)S(1)} %with_inverses.1.after_ref.order_ref), custom_call_target="tpu_custom_call" | custom-call | flops 1073741824 | bytes 4194304 | tf_op jit(solution)/shard_map/turn_backward/pallas_call | solution.py:311
  152.7 13.5 %all_to_all.27.in_ref = bf16[32,32,128]{2,1,0:T(8,128)(2,1)} all-to-all(bf16[32,32,128]{2,1,0:T(8,128)(2,1)S(1)} %bitcast.16), channel_id=1, replica_groups=mesh['z'=16,'xh'=2,'xl'=2,'y'=4,'c'=2] {'xh','xl','y','c'}, dimensions={0} | all-to-all | bytes 524288 | tf_op jit(solution)/shard_map/all_to_all | solution.py:23
  166.2 1.6 sum_copies.1
  167.9 23.5 %all_to_all.28 = bf16[16,32,128]{2,1,0:T(8,128)(2,1)S(1)} all-to-all(bf16[16,32,128]{2,1,0:T(8,128)(2,1)} %sum_copies.1), channel_id=1, replica_groups=mesh['z'=16,'xh'=2,'xl'=2,'y'=4,'c'=2] {'z'}, dimensions={0} | all-to-all | bytes 262144 | tf_op jit(solution)/shard_map/all_to_all | solution.py:23
  191.4 0.6 reshape.43
  192.0 0.0 reduce-scatter.5.cloned.1.call-done
  (1 shorter events, 0.0 us)
Async XLA Ops:
  7.2 23.2 %copy-start.5 = (s32[4,1024]{1,0:T(4,128)S(1)}, s32[4,1024]{1,0:T(4,128)}, u32[]{:S(2)}) copy-start(s32[4,1024]{1,0:T(4,128)} %row_ref.1) | copy-start | bytes 49156
  7.2 25.9 %copy-start = (bf16[832,1024]{1,0:T(8,128)(2,1)S(1)}, bf16[832,1024]{1,0:T(8,128)(2,1)}, u32[]{:S(2)}) copy-start(bf16[832,1024]{1,0:T(8,128)(2,1)} %weight_ref.5) | copy-start | bytes 5111812
  7.2 118.1 %reduce-scatter.3.cloned.1.call-start = ((), (), s32[]{:S(2)}) async-start(), calls=%async_computation.7 | async-start | bytes 2228224 | tf_op jit(solution)/shard_map/reduce_scatter | solution.py:495
  28.4 4.7 %collective-permute-start = (bf16[8,64,960]{2,1,0:T(8,128)(2,1)S(1)}, bf16[8,64,960]{2,1,0:T(8,128)(2,1)}, u32[]{:S(2)}, u32[]{:S(2)}) collective-permute-start(bf16[8,64,960]{2,1,0:T(8,128)(2,1)S(1)} %all_to_all.25.own_ref), channel_id=1, source_target_pairs={{0,1},{1,0},{2,3},{3,2},{4,5},{5,4},{6,7},{7,6},{8,9},{9,8},{10,11... | collective-permute-start | bytes 2949128 | tf_op jit(solution)/shard_map/ppermute | solution.py:492
  44.1 0.7 copy-start.8
  44.8 74.9 %copy-start.6 = (f32[4,32,1024]{2,1,0:T(8,128)}, f32[4,32,1024]{2,1,0:T(8,128)S(1)}, u32[]{:S(2)}) copy-start(f32[4,32,1024]{2,1,0:T(8,128)S(1)} %get-tuple-element.7.trig_ref) | copy-start | bytes 1572868
  44.8 13.1 %all-to-all-start.1 = ((bf16[32,16,128]{2,1,0:T(8,128)(2,1)}), bf16[32,16,128]{2,1,0:T(8,128)(2,1)S(1)}, u32[]{:S(2)}, u32[]{:S(2)}) async-start(bf16[32,16,128]{2,1,0:T(8,128)(2,1)} %bitcast.2), calls=%async_computation.1 | async-start | bytes 262144 | tf_op jit(solution)/shard_map/all_to_all | solution.py:23
  51.9 140.2 %reduce-scatter.5.cloned.1.call-start = ((), (), s32[]{:S(2)}) async-start(), calls=%async_computation.8 | async-start | bytes 1032192 | tf_op jit(solution)/shard_map/reduce_scatter | solution.py:512
  57.9 0.7 copy-start.10
  119.4 1.5 copy-start.1
  123.4 4.6 %collective-permute-start.1 = (bf16[8,64,832]{2,1,0:T(8,128)(2,1)}, bf16[8,64,832]{2,1,0:T(8,128)(2,1)S(1)}, u32[]{:S(2)}, u32[]{:S(2)}) collective-permute-start(bf16[8,64,832]{2,1,0:T(8,128)(2,1)} %projected_half.2), channel_id=1, source_target_pairs={{0,1},{1,0},{2,3},{3,2},{4,5},{5,4},{6,7},{7,6},{8,9},{9,8},{10,11... | collective-permute-start | bytes 2555912 | tf_op jit(solution)/shard_map/ppermute | solution.py:510
  127.9 1.5 copy-start.2
  129.4 0.9 copy-start.3
  130.3 2.6 %copy-start.4 = (bf16[2,16,16,128]{3,2,1,0:T(8,128)(2,1)S(1)}, bf16[2,16,16,128]{3,2,1,0:T(8,128)(2,1)}, u32[]{:S(2)}) copy-start(bf16[2,16,16,128]{3,2,1,0:T(8,128)(2,1)} %spread.1.refs_1_) | copy-start | bytes 393220
  146.8 1.1 copy-start.7
  147.8 1.0 copy-start.9
Sparse Core Ops, SparseCore 0:
  37.8 80.9 reduce-scatter.2
  133.0 43.6 reduce-scatter.4

commit v4 on v3

--- a/solution.py
+++ b/solution.py
@@ -397,8 +397,7 @@
     )(array)
 
 
-def projected_kernel(core_ref, token_ref, exponent_ref, weight_ref, *refs):
-    out_ref = refs[-1]
+def projected_kernel(core_ref, token_ref, exponent_ref, weight_ref, out_ref):
     near, _, few, lanes = token_ref.shape
     width = weight_ref.shape[1]
     parts = lanes // width
@@ -419,13 +418,10 @@
     for part in range(parts):
         piece = (out[part * near * few : (part + 1) * near * few] * scale).astype(BF16)
         piece = piece.reshape(near, few, piece.shape[1])
-        rows = slice(part * few, (part + 1) * few)
-        if len(refs) > 1:
-            piece = (piece.astype(F32) + refs[0][:, rows].astype(F32)).astype(BF16)
-        out_ref[:, rows] = piece
-
-
-def projected_half(core, token_all, weight, each, arrived=None, after=None):
+        out_ref[:, part * few : (part + 1) * few] = piece
+
+
+def projected_half(core, token_all, weight, each):
     near, _, few, _ = token_all.shape
     hidden, width = weight.shape
     steps = 2
@@ -436,11 +432,6 @@
         pl.BlockSpec((hidden, width), lambda e, c: (0, 0)),
     ]
     operands = [core, token_all, token_all, weight]
-    if arrived is not None:
-        in_specs.append(pl.BlockSpec((near, at_once * few, hidden), lambda e, c: (0, e, 0)))
-        operands.append(arrived)
-        in_specs.append(pl.BlockSpec(memory_space=pl.ANY))
-        operands.append(after)
     return pl.pallas_call(
         projected_kernel,
         grid_spec=pltpu.PrefetchScalarGridSpec(
@@ -504,15 +495,15 @@
     token_all = lax.all_gather(back, Z, axis=0, tiled=True).astype(BF16)
     token_all = token_all.reshape(near, 2, groups, each * width + LANES)
 
-    g = spread(summed, sides, groups)
-
     sent = projected_half(1 - core, token_all, up_weight, each)
     arrived = lax.ppermute(sent, "c", other_core)
-    both = projected_half(core, token_all, up_weight, each, arrived, g)
+    both = projected_half(core, token_all, up_weight, each)
+    both = (both.astype(F32) + arrived.astype(F32)).astype(BF16)
     projected = lax.psum_scatter(
         both.reshape(near * each * groups, hidden), NEAR, scatter_dimension=0, tiled=True
     )
 
+    g = spread(summed, sides, groups)
     g = all_to_all(g.reshape((sides * groups,) + g.shape[2:]), PLANE).reshape(rotated.shape)
     sums = turn_backward(strides, groups, own_rows, sides, g, kept, trig, order)
 

time: 200 us -> 194 us (0.970)
  local copies, waits for them, and re-layouts: 7.76 us -> 2.2 us
    unnamed x23 -> x11, local copies, waits for them, and re-layouts: 7.15 us -> 1.58 us
  transfers between devices with their start and end apart: 5 -> 5, of which waited for: 3 -> 3; matrix products, arithmetic and copies ran while one was open for 1% -> 2% of each run, Pallas kernels for 10% -> 11%
where the time goes in v4:
time: 194 us; the launch traced here: 193 us
  blocking collectives  128 us (66%)
  Pallas kernels  28.1 us (14%)
  between operations  14.2 us (7%)
  starting transfers between devices  11 us (6%)
  waiting for transfers between devices  7.13 us (4%)
  other arithmetic  2.38 us (1%)
  local copies, waits for them, and re-layouts  2.2 us (1%)
    all_to_all x4, blocking collectives, all_to_all(): return lax.all_to_all(array, axes, 0, 0, tiled=True)  70.6 us
    all_gather x1, blocking collectives, per_device(): token_all = lax.all_gather(back, Z, axis=0, tiled=True).astype(BF16)  57.5 us
    all_to_all x1, starting transfers between devices, all_to_all(): return lax.all_to_all(array, axes, 0, 0, tiled=True)  7.07 us
    pallas_call x1, Pallas kernels, turn_forward(): pl.pallas_call(functools.partial(forward_kernel, strides, groups, each),...  6.42 us
    all_to_all x1, waiting for transfers between devices, all_to_all(): return lax.all_to_all(array, axes, 0, 0, tiled=True)  6.01 us
    pallas_call x1, Pallas kernels, gradient(): pl.pallas_call(gradient_kernel, grid=(steps,), in_specs=[pl.BlockSpec(mem...  4.63 us
    pallas_call x1, Pallas kernels, turn_backward(): pl.pallas_call(functools.partial(backward_kernel, strides, groups, each),...  3.93 us
  transfers between devices with their start and end apart: 5, of which 3 were waited for; matrix products, arithmetic and copies ran while one was open for 2% of the time, Pallas kernels for 11%

profile of v4, /device:TPU:24, one launch (start us, length us, event | category | flops | bytes accessed | tf_op | source)
XLA Modules:
  0.0 193.1 jit_solution(1997400019938252119)
XLA Ops:
  7.2 0.0 copy-start.1
  7.2 0.0 reduce-scatter.5.cloned.1.call-start
  7.2 2.2 %prepare.1 = bf16[8,64,960]{2,1,0:T(8,128)(2,1)} custom-call(bf16[32,1024]{1,0:T(8,128)(2,1)} %token_ref.1, f32[4,1024]{1,0:T(4,128)} %angle_ref.1, bf16[64,832]{1,0:T(8,128)(2,1)} %cot_ref.1), custom_call_target="tpu_custom_call" | custom-call | tf_op jit(solution)/shard_map/prepare/pallas_call | solution.py:96
  9.4 0.0 copy-start
  9.4 19.0 %all_to_all.25.own_ref = bf16[8,64,960]{2,1,0:T(8,128)(2,1)S(1)} all-to-all(bf16[8,64,960]{2,1,0:T(8,128)(2,1)} %prepare.1), channel_id=1, replica_groups=mesh['z'=16,'xh'=2,'xl'=2,'y'=4,'c'=2] {'xl','y'}, dimensions={0} | all-to-all | bytes 1966080 | tf_op jit(solution)/shard_map/all_to_all | solution.py:23
  28.4 1.9 collective-permute-start
  30.3 0.0 copy-done.1
  30.3 0.2 copy.7
  30.6 2.1 %with_inverses.1.after_ref.order_ref = s32[4,2,1024]{2,1,0:T(2,128)S(1)} custom-call(s32[1024,4]{1,0:T(8,128)S(1)} %bitcast.14, s32[4,1024]{1,0:T(4,128)S(1)} %copy-done.1), custom_call_target="tpu_custom_call" | custom-call | tf_op jit(solution)/shard_map/with_inverses/pallas_call | solution.py:64
  32.7 0.4 collective-permute-done.other_ref
  33.1 0.0 copy-done
  33.1 4.6 %gradient.1.after_ref = bf16[8,2,64,1024]{3,2,1,0:T(8,128)(2,1)} custom-call(s32[1]{0:T(128)} %bitcast.core_ref, bf16[8,64,960]{2,1,0:T(8,128)(2,1)S(1)} %all_to_all.25.own_ref, bf16[8,64,960]{2,1,0:T(8,128)(2,1)} %collective-permute-done.other_ref, bf16[832,1024]{1,0:T(8,128)(2,1)S(1)} %copy-done, s32[4,2,1024]{2,1,0:T(2,128)S(1)} %with_inverses.1.after_ref.order_ref), custom_call_target="tpu_custom_call" | custom-call | flops 1744830464 | bytes 6291456 | tf_op jit(solution)/shard_map/gradient/pallas_call | solution.py:355
  37.7 0.0 reduce-scatter.5.cloned.1.call-update
  37.7 6.4 %turn_forward.1 = (bf16[2,16,16,128]{3,2,1,0:T(8,128)(2,1)}, bf16[4,32,1024]{2,1,0:T(8,128)(2,1)S(1)}, f32[4,32,1024]{2,1,0:T(8,128)S(1)}) custom-call(s32[1]{0:T(128)} %bitcast.core_ref, bf16[8,64,960]{2,1,0:T(8,128)(2,1)S(1)} %all_to_all.25.own_ref, bf16[8,64,960]{2,1,0:T(8,128)(2,1)} %collective-permute-done.other_ref, ...), custom_call_target="tpu_custom_call" | custom-call | flops 1073741824 | bytes 4194304 | tf_op jit(solution)/shard_map/turn_forward/pallas_call | solution.py:273
  44.2 0.0 copy-start.2
  44.2 0.7 copy-done.2
  44.9 7.1 %all-to-all-start.1 = ((bf16[32,16,128]{2,1,0:T(8,128)(2,1)}), bf16[32,16,128]{2,1,0:T(8,128)(2,1)S(1)}, u32[]{:S(2)}, u32[]{:S(2)}) async-start(bf16[32,16,128]{2,1,0:T(8,128)(2,1)} %bitcast.2), calls=%async_computation.1 | async-start | bytes 262144 | tf_op jit(solution)/shard_map/all_to_all | solution.py:23
  51.9 0.0 reduce-scatter.3.cloned.1.call-start
  52.0 6.0 %all-to-all-done.1 = bf16[32,16,128]{2,1,0:T(8,128)(2,1)S(1)} async-done(((bf16[32,16,128]{2,1,0:T(8,128)(2,1)}), bf16[32,16,128]{2,1,0:T(8,128)(2,1)S(1)}, u32[]{:S(2)}, u32[]{:S(2)}) %all-to-all-start.1) | async-done | bytes 131104 | tf_op jit(solution)/shard_map/all_to_all | solution.py:23
  58.0 0.0 copy-start.4
  58.0 0.6 copy-done.4
  58.6 1.9 %pack.1 = bf16[16,4224]{1,0:T(8,128)(2,1)} custom-call(bf16[2,16,16,128]{3,2,1,0:T(8,128)(2,1)} %bitcast.18), custom_call_target="tpu_custom_call" | custom-call | tf_op jit(solution)/shard_map/pack/pallas_call | solution.py:214
  60.6 0.9 convert_element_type.18
  61.5 57.5 %all-gather.1 = f16[256,4224]{1,0:T(8,128)(2,1)S(1)} all-gather(f16[16,4224]{1,0:T(8,128)(2,1)S(1)} %convert_element_type.18), channel_id=1, replica_groups=mesh['z'=16,'xh'=2,'xl'=2,'y'=4,'c'=2] {'z'}, dimensions={0}, use_global_device_ids=true | all-gather | bytes 2297856 | tf_op jit(solution)/shard_map/all_gather | solution.py:495
  119.1 0.2 convert_element_type.19
  119.3 1.8 projected_half.3
  121.1 1.9 collective-permute-start.1
  123.0 1.8 projected_half.2
  124.8 0.0 copy-start.3
  124.8 0.7 collective-permute-done.1
  125.4 1.2 add_convert_fusion
  126.6 0.0 reduce-scatter.3.cloned.1.call-update
  126.7 0.0 reduce-scatter.5.cloned.1.call-done.in_ref
  126.7 1.7 spread.1
  128.4 14.2 %all_to_all.26 = bf16[32,16,128]{2,1,0:T(8,128)(2,1)S(1)} all-to-all(bf16[32,16,128]{2,1,0:T(8,128)(2,1)} %bitcast.19), channel_id=1, replica_groups=mesh['z'=16,'xh'=2,'xl'=2,'y'=4,'c'=2] {'xh','xl','y','c'}, dimensions={0} | all-to-all | bytes 262144 | tf_op jit(solution)/shard_map/all_to_all | solution.py:23
  142.6 0.0 copy-done.3
  142.6 3.9 %turn_backward.1 = bf16[2,16,32,128]{3,2,1,0:T(8,128)(2,1)S(1)} custom-call(bf16[2,16,16,128]{3,2,1,0:T(8,128)(2,1)S(1)} %bitcast.16, bf16[4,32,1024]{2,1,0:T(8,128)(2,1)S(1)} %copy-done.3, f32[4,32,1024]{2,1,0:T(8,128)S(1)} %get-tuple-element.7.trig_ref, s32[4,2,1024]{2,1,0:T(2,128)S(1)} %with_inverses.1.after_ref.order_ref), custom_call_target="tpu_custom_call" | custom-call | flops 1073741824 | bytes 4194304 | tf_op jit(solution)/shard_map/turn_backward/pallas_call | solution.py:311
  146.6 13.6 %all_to_all.27.in_ref = bf16[32,32,128]{2,1,0:T(8,128)(2,1)} all-to-all(bf16[32,32,128]{2,1,0:T(8,128)(2,1)S(1)} %bitcast.15), channel_id=1, replica_groups=mesh['z'=16,'xh'=2,'xl'=2,'y'=4,'c'=2] {'xh','xl','y','c'}, dimensions={0} | all-to-all | bytes 524288 | tf_op jit(solution)/shard_map/all_to_all | solution.py:23
  160.2 1.6 sum_copies.1
  161.8 23.8 %all_to_all.28 = bf16[16,32,128]{2,1,0:T(8,128)(2,1)S(1)} all-to-all(bf16[16,32,128]{2,1,0:T(8,128)(2,1)} %sum_copies.1), channel_id=1, replica_groups=mesh['z'=16,'xh'=2,'xl'=2,'y'=4,'c'=2] {'z'}, dimensions={0} | all-to-all | bytes 262144 | tf_op jit(solution)/shard_map/all_to_all | solution.py:23
  185.7 0.6 reshape.43
  186.3 0.0 reduce-scatter.3.cloned.1.call-done
  (1 shorter events, 0.0 us)
Async XLA Ops:
  7.2 23.2 %copy-start.1 = (s32[4,1024]{1,0:T(4,128)S(1)}, s32[4,1024]{1,0:T(4,128)}, u32[]{:S(2)}) copy-start(s32[4,1024]{1,0:T(4,128)} %row_ref.1) | copy-start | bytes 49156
  7.2 119.5 %reduce-scatter.5.cloned.1.call-start = ((), (), s32[]{:S(2)}) async-start(), calls=%async_computation.8 | async-start | bytes 2228224 | tf_op jit(solution)/shard_map/reduce_scatter | solution.py:486
  9.4 23.6 %copy-start = (bf16[832,1024]{1,0:T(8,128)(2,1)S(1)}, bf16[832,1024]{1,0:T(8,128)(2,1)}, u32[]{:S(2)}) copy-start(bf16[832,1024]{1,0:T(8,128)(2,1)} %weight_ref.5) | copy-start | bytes 5111812
  28.4 4.7 %collective-permute-start = (bf16[8,64,960]{2,1,0:T(8,128)(2,1)S(1)}, bf16[8,64,960]{2,1,0:T(8,128)(2,1)}, u32[]{:S(2)}, u32[]{:S(2)}) collective-permute-start(bf16[8,64,960]{2,1,0:T(8,128)(2,1)S(1)} %all_to_all.25.own_ref), channel_id=1, source_target_pairs={{0,1},{1,0},{2,3},{3,2},{4,5},{5,4},{6,7},{7,6},{8,9},{9,8},{10,11... | collective-permute-start | bytes 2949128 | tf_op jit(solution)/shard_map/ppermute | solution.py:483
  44.2 0.7 copy-start.2
  44.9 13.1 %all-to-all-start.1 = ((bf16[32,16,128]{2,1,0:T(8,128)(2,1)}), bf16[32,16,128]{2,1,0:T(8,128)(2,1)S(1)}, u32[]{:S(2)}, u32[]{:S(2)}) async-start(bf16[32,16,128]{2,1,0:T(8,128)(2,1)} %bitcast.2), calls=%async_computation.1 | async-start | bytes 262144 | tf_op jit(solution)/shard_map/all_to_all | solution.py:23
  51.9 134.4 %reduce-scatter.3.cloned.1.call-start = ((), (), s32[]{:S(2)}) async-start(), calls=%async_computation.7 | async-start | bytes 1032192 | tf_op jit(solution)/shard_map/reduce_scatter | solution.py:502
  58.0 0.6 copy-start.4
  121.1 4.4 %collective-permute-start.1 = (bf16[8,64,832]{2,1,0:T(8,128)(2,1)S(1)}, bf16[8,64,832]{2,1,0:T(8,128)(2,1)S(1)}, u32[]{:S(2)}, u32[]{:S(2)}) collective-permute-start(bf16[8,64,832]{2,1,0:T(8,128)(2,1)S(1)} %projected_half.3), channel_id=1, source_target_pairs={{0,1},{1,0},{2,3},{3,2},{4,5},{5,4},{6,7},{7,6},{8,9},{9,8},{10,11... | collective-permute-start | bytes 2555912 | tf_op jit(solution)/shard_map/ppermute | solution.py:499
  124.8 17.9 %copy-start.3 = (bf16[4,32,1024]{2,1,0:T(8,128)(2,1)S(1)}, bf16[4,32,1024]{2,1,0:T(8,128)(2,1)}, u32[]{:S(2)}) copy-start(bf16[4,32,1024]{2,1,0:T(8,128)(2,1)} %copy-done.2) | copy-start | bytes 786436
Sparse Core Ops, SparseCore 0:
  37.9 80.9 reduce-scatter.4
  126.8 44.0 reduce-scatter.2

commit v5 on v4

--- a/solution.py
+++ b/solution.py
@@ -424,7 +424,7 @@
 def projected_half(core, token_all, weight, each):
     near, _, few, _ = token_all.shape
     hidden, width = weight.shape
-    steps = 2
+    steps = 1
     at_once = each // steps
     in_specs = [
         pl.BlockSpec((near, 1, few, at_once * width), lambda e, c: (0, c[0], 0, e)),

time: 194 us -> 194 us (level)
  no operation moved by 1% of the time
where the time goes in v5:
time: 194 us; the launch traced here: 193 us
  blocking collectives  128 us (66%)
  Pallas kernels  27.2 us (14%)
  between operations  14.2 us (7%)
  starting transfers between devices  11 us (6%)
  waiting for transfers between devices  7.58 us (4%)
  other arithmetic  2.38 us (1%)
  local copies, waits for them, and re-layouts  2.2 us (1%)
    all_to_all x4, blocking collectives, all_to_all(): return lax.all_to_all(array, axes, 0, 0, tiled=True)  70.5 us
    all_gather x1, blocking collectives, per_device(): token_all = lax.all_gather(back, Z, axis=0, tiled=True).astype(BF16)  57.5 us
    all_to_all x1, starting transfers between devices, all_to_all(): return lax.all_to_all(array, axes, 0, 0, tiled=True)  7.07 us
    pallas_call x1, Pallas kernels, turn_forward(): pl.pallas_call(functools.partial(forward_kernel, strides, groups, each),...  6.42 us
    all_to_all x1, waiting for transfers between devices, all_to_all(): return lax.all_to_all(array, axes, 0, 0, tiled=True)  6.01 us
    pallas_call x1, Pallas kernels, gradient(): pl.pallas_call(gradient_kernel, grid=(steps,), in_specs=[pl.BlockSpec(mem...  4.63 us
    pallas_call x1, Pallas kernels, turn_backward(): pl.pallas_call(functools.partial(backward_kernel, strides, groups, each),...  3.93 us
  transfers between devices with their start and end apart: 5, of which 3 were waited for; matrix products, arithmetic and copies ran while one was open for 2% of the time, Pallas kernels for 11%

profile of v5, /device:TPU:24, one launch (start us, length us, event | category | flops | bytes accessed | tf_op | source)
XLA Modules:
  0.0 192.6 jit_solution(5460914170553640947)
XLA Ops:
  7.2 0.0 copy-start.1
  7.2 0.0 reduce-scatter.5.cloned.1.call-start
  7.2 2.2 %prepare.1 = bf16[8,64,960]{2,1,0:T(8,128)(2,1)} custom-call(bf16[32,1024]{1,0:T(8,128)(2,1)} %token_ref.1, f32[4,1024]{1,0:T(4,128)} %angle_ref.1, bf16[64,832]{1,0:T(8,128)(2,1)} %cot_ref.1), custom_call_target="tpu_custom_call" | custom-call | tf_op jit(solution)/shard_map/prepare/pallas_call | solution.py:96
  9.4 0.0 copy-start
  9.4 19.0 %all_to_all.25.own_ref = bf16[8,64,960]{2,1,0:T(8,128)(2,1)S(1)} all-to-all(bf16[8,64,960]{2,1,0:T(8,128)(2,1)} %prepare.1), channel_id=1, replica_groups=mesh['z'=16,'xh'=2,'xl'=2,'y'=4,'c'=2] {'xl','y'}, dimensions={0} | all-to-all | bytes 1966080 | tf_op jit(solution)/shard_map/all_to_all | solution.py:23
  28.4 1.9 collective-permute-start
  30.3 0.0 copy-done.1
  30.3 0.2 copy.7
  30.6 2.1 %with_inverses.1.after_ref.order_ref = s32[4,2,1024]{2,1,0:T(2,128)S(1)} custom-call(s32[1024,4]{1,0:T(8,128)S(1)} %bitcast.14, s32[4,1024]{1,0:T(4,128)S(1)} %copy-done.1), custom_call_target="tpu_custom_call" | custom-call | tf_op jit(solution)/shard_map/with_inverses/pallas_call | solution.py:64
  32.7 0.4 collective-permute-done.other_ref
  33.1 0.0 copy-done
  33.1 4.6 %gradient.1.after_ref = bf16[8,2,64,1024]{3,2,1,0:T(8,128)(2,1)} custom-call(s32[1]{0:T(128)} %bitcast.core_ref, bf16[8,64,960]{2,1,0:T(8,128)(2,1)S(1)} %all_to_all.25.own_ref, bf16[8,64,960]{2,1,0:T(8,128)(2,1)} %collective-permute-done.other_ref, bf16[832,1024]{1,0:T(8,128)(2,1)S(1)} %copy-done, s32[4,2,1024]{2,1,0:T(2,128)S(1)} %with_inverses.1.after_ref.order_ref), custom_call_target="tpu_custom_call" | custom-call | flops 1744830464 | bytes 6291456 | tf_op jit(solution)/shard_map/gradient/pallas_call | solution.py:355
  37.7 0.0 reduce-scatter.5.cloned.1.call-update
  37.7 6.4 %turn_forward.1 = (bf16[2,16,16,128]{3,2,1,0:T(8,128)(2,1)}, bf16[4,32,1024]{2,1,0:T(8,128)(2,1)S(1)}, f32[4,32,1024]{2,1,0:T(8,128)S(1)}) custom-call(s32[1]{0:T(128)} %bitcast.core_ref, bf16[8,64,960]{2,1,0:T(8,128)(2,1)S(1)} %all_to_all.25.own_ref, bf16[8,64,960]{2,1,0:T(8,128)(2,1)} %collective-permute-done.other_ref, ...), custom_call_target="tpu_custom_call" | custom-call | flops 1073741824 | bytes 4194304 | tf_op jit(solution)/shard_map/turn_forward/pallas_call | solution.py:273
  44.2 0.0 copy-start.2
  44.2 0.7 copy-done.2
  44.9 7.1 %all-to-all-start.1 = ((bf16[32,16,128]{2,1,0:T(8,128)(2,1)}), bf16[32,16,128]{2,1,0:T(8,128)(2,1)S(1)}, u32[]{:S(2)}, u32[]{:S(2)}) async-start(bf16[32,16,128]{2,1,0:T(8,128)(2,1)} %bitcast.2), calls=%async_computation.1 | async-start | bytes 262144 | tf_op jit(solution)/shard_map/all_to_all | solution.py:23
  51.9 0.0 reduce-scatter.3.cloned.1.call-start
  52.0 6.0 %all-to-all-done.1 = bf16[32,16,128]{2,1,0:T(8,128)(2,1)S(1)} async-done(((bf16[32,16,128]{2,1,0:T(8,128)(2,1)}), bf16[32,16,128]{2,1,0:T(8,128)(2,1)S(1)}, u32[]{:S(2)}, u32[]{:S(2)}) %all-to-all-start.1) | async-done | bytes 131104 | tf_op jit(solution)/shard_map/all_to_all | solution.py:23
  58.0 0.0 copy-start.4
  58.0 0.6 copy-done.4
  58.6 1.9 %pack.1 = bf16[16,4224]{1,0:T(8,128)(2,1)} custom-call(bf16[2,16,16,128]{3,2,1,0:T(8,128)(2,1)} %bitcast.18), custom_call_target="tpu_custom_call" | custom-call | tf_op jit(solution)/shard_map/pack/pallas_call | solution.py:214
  60.6 0.9 convert_element_type.18
  61.5 57.5 %all-gather.1 = f16[256,4224]{1,0:T(8,128)(2,1)S(1)} all-gather(f16[16,4224]{1,0:T(8,128)(2,1)S(1)} %convert_element_type.18), channel_id=1, replica_groups=mesh['z'=16,'xh'=2,'xl'=2,'y'=4,'c'=2] {'z'}, dimensions={0}, use_global_device_ids=true | all-gather | bytes 2297856 | tf_op jit(solution)/shard_map/all_gather | solution.py:495
  119.1 0.2 convert_element_type.19
  119.3 1.3 projected_half.3
  120.6 1.9 collective-permute-start.1
  122.6 1.3 projected_half.2
  123.9 0.0 copy-start.3
  123.9 1.1 collective-permute-done.1
  125.0 1.2 add_convert_fusion
  126.2 0.0 reduce-scatter.3.cloned.1.call-update
  126.2 0.0 reduce-scatter.5.cloned.1.call-done.in_ref
  126.2 1.7 spread.1
  128.0 14.2 %all_to_all.26 = bf16[32,16,128]{2,1,0:T(8,128)(2,1)S(1)} all-to-all(bf16[32,16,128]{2,1,0:T(8,128)(2,1)} %bitcast.19), channel_id=1, replica_groups=mesh['z'=16,'xh'=2,'xl'=2,'y'=4,'c'=2] {'xh','xl','y','c'}, dimensions={0} | all-to-all | bytes 262144 | tf_op jit(solution)/shard_map/all_to_all | solution.py:23
  142.2 0.0 copy-done.3
  142.2 3.9 %turn_backward.1 = bf16[2,16,32,128]{3,2,1,0:T(8,128)(2,1)S(1)} custom-call(bf16[2,16,16,128]{3,2,1,0:T(8,128)(2,1)S(1)} %bitcast.16, bf16[4,32,1024]{2,1,0:T(8,128)(2,1)S(1)} %copy-done.3, f32[4,32,1024]{2,1,0:T(8,128)S(1)} %get-tuple-element.7.trig_ref, s32[4,2,1024]{2,1,0:T(2,128)S(1)} %with_inverses.1.after_ref.order_ref), custom_call_target="tpu_custom_call" | custom-call | flops 1073741824 | bytes 4194304 | tf_op jit(solution)/shard_map/turn_backward/pallas_call | solution.py:311
  146.1 13.6 %all_to_all.27.in_ref = bf16[32,32,128]{2,1,0:T(8,128)(2,1)} all-to-all(bf16[32,32,128]{2,1,0:T(8,128)(2,1)S(1)} %bitcast.15), channel_id=1, replica_groups=mesh['z'=16,'xh'=2,'xl'=2,'y'=4,'c'=2] {'xh','xl','y','c'}, dimensions={0} | all-to-all | bytes 524288 | tf_op jit(solution)/shard_map/all_to_all | solution.py:23
  159.7 1.6 sum_copies.1
  161.4 23.7 %all_to_all.28 = bf16[16,32,128]{2,1,0:T(8,128)(2,1)S(1)} all-to-all(bf16[16,32,128]{2,1,0:T(8,128)(2,1)} %sum_copies.1), channel_id=1, replica_groups=mesh['z'=16,'xh'=2,'xl'=2,'y'=4,'c'=2] {'z'}, dimensions={0} | all-to-all | bytes 262144 | tf_op jit(solution)/shard_map/all_to_all | solution.py:23
  185.1 0.6 reshape.43
  185.7 0.0 reduce-scatter.3.cloned.1.call-done
  (1 shorter events, 0.0 us)
Async XLA Ops:
  7.2 23.2 %copy-start.1 = (s32[4,1024]{1,0:T(4,128)S(1)}, s32[4,1024]{1,0:T(4,128)}, u32[]{:S(2)}) copy-start(s32[4,1024]{1,0:T(4,128)} %row_ref.1) | copy-start | bytes 49156
  7.2 119.1 %reduce-scatter.5.cloned.1.call-start = ((), (), s32[]{:S(2)}) async-start(), calls=%async_computation.8 | async-start | bytes 2228224 | tf_op jit(solution)/shard_map/reduce_scatter | solution.py:486
  9.4 23.6 %copy-start = (bf16[832,1024]{1,0:T(8,128)(2,1)S(1)}, bf16[832,1024]{1,0:T(8,128)(2,1)}, u32[]{:S(2)}) copy-start(bf16[832,1024]{1,0:T(8,128)(2,1)} %weight_ref.5) | copy-start | bytes 5111812
  28.4 4.7 %collective-permute-start = (bf16[8,64,960]{2,1,0:T(8,128)(2,1)S(1)}, bf16[8,64,960]{2,1,0:T(8,128)(2,1)}, u32[]{:S(2)}, u32[]{:S(2)}) collective-permute-start(bf16[8,64,960]{2,1,0:T(8,128)(2,1)S(1)} %all_to_all.25.own_ref), channel_id=1, source_target_pairs={{0,1},{1,0},{2,3},{3,2},{4,5},{5,4},{6,7},{7,6},{8,9},{9,8},{10,11... | collective-permute-start | bytes 2949128 | tf_op jit(solution)/shard_map/ppermute | solution.py:483
  44.2 0.7 copy-start.2
  44.9 13.1 %all-to-all-start.1 = ((bf16[32,16,128]{2,1,0:T(8,128)(2,1)}), bf16[32,16,128]{2,1,0:T(8,128)(2,1)S(1)}, u32[]{:S(2)}, u32[]{:S(2)}) async-start(bf16[32,16,128]{2,1,0:T(8,128)(2,1)} %bitcast.2), calls=%async_computation.1 | async-start | bytes 262144 | tf_op jit(solution)/shard_map/all_to_all | solution.py:23
  51.9 133.8 %reduce-scatter.3.cloned.1.call-start = ((), (), s32[]{:S(2)}) async-start(), calls=%async_computation.7 | async-start | bytes 1032192 | tf_op jit(solution)/shard_map/reduce_scatter | solution.py:502
  58.0 0.6 copy-start.4
  120.6 4.4 %collective-permute-start.1 = (bf16[8,64,832]{2,1,0:T(8,128)(2,1)S(1)}, bf16[8,64,832]{2,1,0:T(8,128)(2,1)S(1)}, u32[]{:S(2)}, u32[]{:S(2)}) collective-permute-start(bf16[8,64,832]{2,1,0:T(8,128)(2,1)S(1)} %projected_half.3), channel_id=1, source_target_pairs={{0,1},{1,0},{2,3},{3,2},{4,5},{5,4},{6,7},{7,6},{8,9},{9,8},{10,11... | collective-permute-start | bytes 2555912 | tf_op jit(solution)/shard_map/ppermute | solution.py:499
  123.9 18.3 %copy-start.3 = (bf16[4,32,1024]{2,1,0:T(8,128)(2,1)S(1)}, bf16[4,32,1024]{2,1,0:T(8,128)(2,1)}, u32[]{:S(2)}) copy-start(bf16[4,32,1024]{2,1,0:T(8,128)(2,1)} %copy-done.2) | copy-start | bytes 786436
Sparse Core Ops, SparseCore 0:
  37.9 80.9 reduce-scatter.4
  126.3 44.0 reduce-scatter.2
